TPU v7x, 32 devices: a whole 2x2x4 slice. The times are simulated.
32 devices in a mesh: dp: 4 (over y, x), expert: 8 (over z, core).
Axes of the slice: x: 2, y: 2, z: 4, core: 2. Of those that a mesh axis runs over, the one named last changes fastest.
Arguments:
- tokens: bfloat16 [2048, 4096], P(('dp', 'expert')), may hold values from -6 to 6
- routes: int32 [2048, 8], P(('dp', 'expert')), may hold values from 0 to 15, all different within a row; in each aligned block of 64 rows (0 to 63, 64 to 127, ...) at most 42 rows name the same one
- gate_fixed: int32 [2048, 8], P(('dp', 'expert')), may hold values from 1 to 65535
- w_gate: bfloat16 [32, 4096, 768], P(('dp', 'expert')), may hold values from -0.09375 to 0.09375
- w_up: bfloat16 [32, 4096, 768], P(('dp', 'expert')), may hold values from -0.09375 to 0.09375
- w_down: bfloat16 [32, 768, 4096], P(('dp', 'expert')), may hold values from -0.15625 to 0.15625
Outputs:
- mixed: bfloat16 [2048, 4096], P(('dp', 'expert'))
Inputs may be any that keep to these rules, and one draw needn't show every extreme that they name: `routes`: each row names 8 different experts. In each aligned block of 64 rows (the rows of one device) no expert is named by more than 42 rows, and in some block one expert is named by exactly 42 rows.
All inputs are finite; a program needn't handle non-finite values.
Results may differ from a plain program's by a relative error of at most 0.0058.
Values may be sent and summed in bfloat16 or wider, within the bound.
No kernel may reach another device: no remote copies, remote signals or barrier semaphores. Data moves between devices by JAX's collectives and lax.ppermute only.
A program may use at most 192 MiB of HBM per device.

v0:
```python
import jax
import jax.numpy as jnp
from jax import lax
from jax.sharding import PartitionSpec as P

TOP = 8


def from_partner(block, axis, stride):
    count = lax.axis_size(axis)
    route = []
    for low in range(count):
        high = low | 1 << stride
        if high != low and high < count:
            route += [(low, high), (high, low)]
    return lax.ppermute(block, axis, route)


def half_hidden(rows, gate_part, up_part):
    gate = jnp.dot(rows, gate_part, preferred_element_type=jnp.float32)
    upper = jnp.dot(rows, up_part, preferred_element_type=jnp.float32)
    return (jax.nn.silu(gate) * upper).astype(jnp.bfloat16)


def on_device(tokens, routes, gate_fixed, w_gate, w_up, w_down):
    n_data = lax.axis_size("dp")
    n_owner = lax.axis_size("expert")
    devices_all = n_data * n_owner
    expert_count = devices_all // 2
    tok_rows = tokens.shape[0]
    width = tokens.shape[1]
    capacity = 2 * (5 * tok_rows * TOP // (8 * expert_count) + 1)
    per_half = capacity // 2
    quant = gate_fixed.astype(jnp.float32)
    weights = quant / jnp.sum(quant, axis=1, keepdims=True)
    flat_routes = routes.reshape(-1)
    onehot = (flat_routes[:, None] == jnp.arange(expert_count, dtype=jnp.int32)[None, :]).astype(
        jnp.int32
    )
    before = jnp.cumsum(onehot, axis=0) - onehot
    slot = jnp.sum(before * onehot, axis=1)
    source_rows = jnp.arange(tok_rows * TOP, dtype=jnp.int32) // TOP
    gate_mine = w_gate[0]
    up_mine = w_up[0]
    down_mine = w_down[0]
    parity = lax.axis_index("expert") % 2
    target = 2 * flat_routes + (slot + parity) % 2
    place = target * per_half + slot // 2
    outgoing = (
        jnp.zeros((devices_all * per_half, width), jnp.bfloat16).at[place].set(tokens[source_rows])
    )
    arrived = lax.all_to_all(
        outgoing.reshape(devices_all, per_half, width),
        ("dp", "expert"),
        split_axis=0,
        concat_axis=0,
        tiled=True,
    )
    partner = from_partner(arrived, "expert", 0)
    rows = jnp.concatenate([arrived, partner], axis=0).reshape(-1, width)
    partial_out = jnp.dot(
        half_hidden(rows, gate_mine, up_mine), down_mine, preferred_element_type=jnp.float32
    )
    partial_out = partial_out.reshape(2, devices_all, per_half, width)
    total = partial_out[0] + from_partner(partial_out[1], "expert", 0)
    results = total.astype(jnp.bfloat16)
    returned = lax.all_to_all(
        results, ("dp", "expert"), split_axis=0, concat_axis=0, tiled=True
    ).reshape(-1, width)
    picked = returned[place].astype(jnp.float32).reshape(tok_rows, TOP, width)
    mixed = jnp.sum(weights[:, :, None] * picked, axis=1)
    return mixed.astype(jnp.bfloat16)


def solution(mesh):
    placed = (
        P(("dp", "expert"), None),
        P(("dp", "expert"), None),
        P(("dp", "expert"), None),
        P(("dp", "expert"), None, None),
        P(("dp", "expert"), None, None),
        P(("dp", "expert"), None, None),
    )
    return jax.shard_map(
        on_device, mesh=mesh, in_specs=placed, out_specs=P(("dp", "expert"), None), check_vma=False
    )
```

profile of v0, /device:TPU:0, one launch (start us, length us, event | category | flops | bytes accessed | tf_op | source)
XLA Modules:
  0.0 493.6 jit_solution(5291630096305718043)
XLA Ops:
  0.0 0.8 copy.15
  0.8 0.1 eq.33
  0.9 0.1 eq.29
  1.0 0.7 broadcast_multiply_fusion
  1.7 1.2 reduce-window.6
  2.9 0.2 slice_reduce_fusion
  3.2 0.1 mul.52
  3.3 0.1 fusion.14
  3.5 21.8 %scatter_custom_fusion = bf16[672,4096]{1,0:T(8,128)(2,1)} fusion(s32[512]{0:T(512)S(1)} %bitcast.36, bf16[64,4096]{1,0:T(8,128)(2,1)S(1)} %copy-done, s32[1024]{0:T(1024)S(1)} %pad_clamp_fusion.1, bf16[]{:T(256)} %constant.57.clone.1), kind=kCustom, calls=%fused_computation.14 | custom fusion | bytes 5505026 | tf_op jit(solution)/shard_map/scatter | solution.py:50
  25.3 6.3 %reshape.197 = bf16[32,21,4096]{2,1,0:T(8,128)(2,1)} reshape(bf16[672,4096]{1,0:T(8,128)(2,1)} %scatter_custom_fusion) | data formatting | bytes 11010048 | tf_op jit(solution)/shard_map/reshape | solution.py:53
  31.6 147.7 %all_to_all.10 = bf16[32,21,4096]{2,1,0:T(8,128)(2,1)S(1)} all-to-all(bf16[32,21,4096]{2,1,0:T(8,128)(2,1)} %reshape.197), channel_id=1, replica_groups=mesh['dp'=4,'expert'=8] {'dp','expert'}, dimensions={0} | all-to-all | bytes 11010048 | tf_op jit(solution)/shard_map/all_to_all | solution.py:52
  179.3 3.2 copy.18
  182.6 9.0 %collective-permute-done = bf16[32,21,4096]{2,0,1:T(8,128)(2,1)S(1)} collective-permute-done((bf16[32,21,4096]{2,0,1:T(8,128)(2,1)S(1)}, bf16[32,21,4096]{2,0,1:T(8,128)(2,1)S(1)}, u32[]{:S(2)}, u32[]{:S(2)}) %collective-permute-start) | collective-permute-done | bytes 5505056 | tf_op jit(solution)/shard_map/ppermute | solution.py:16
  191.6 3.0 copy.19
  194.6 6.0 %pad_maximum_fusion = bf16[64,21,4096]{2,1,0:T(8,128)(2,1)} fusion(bf16[32,21,4096]{2,1,0:T(8,128)(2,1)S(1)} %copy.19, bf16[32,21,4096]{2,1,0:T(8,128)(2,1)S(1)} %all_to_all.10), kind=kLoop, calls=%fused_computation.3 | loop fusion | flops 5505024 | bytes 22020096 | tf_op jit(solution)/shard_map/concatenate | solution.py:60
  200.6 12.1 %reshape.198 = bf16[1344,4096]{1,0:T(8,128)(2,1)} reshape(bf16[64,21,4096]{2,1,0:T(8,128)(2,1)} %pad_maximum_fusion) | data formatting | bytes 22020096 | tf_op jit(solution)/shard_map/reshape | solution.py:60
  212.7 12.8 %fusion.4 = f32[1344,768]{1,0:T(8,128)S(1)} fusion(bf16[1344,4096]{1,0:T(8,128)(2,1)} %reshape.198, bf16[1,4096,768]{2,1,0:T(8,128)(2,1)} %param.10), kind=kOutput, calls=%fused_computation.10 | convolution fusion | flops 8455716864 | bytes 21430272 | tf_op jit(solution)/shard_map/dot_general | solution.py:21
  225.5 13.8 %fusion.6 = f32[1344,768]{1,0:T(8,128)S(1)} fusion(bf16[1344,4096]{1,0:T(8,128)(2,1)S(1)} %copy-done.2, bf16[1,4096,768]{2,1,0:T(8,128)(2,1)} %param.9), kind=kOutput, calls=%fused_computation.12 | convolution fusion | flops 8455716864 | bytes 21430272 | tf_op jit(solution)/shard_map/dot_general | solution.py:20
  239.4 12.3 %fusion.2 = f32[1344,4096]{1,0:T(8,128)} fusion(bf16[1,768,4096]{2,1,0:T(8,128)(2,1)S(1)} %bitcast.41, f32[1344,768]{1,0:T(8,128)S(1)} %fusion.4, f32[1344,768]{1,0:T(8,128)S(1)} %fusion.6), kind=kOutput, calls=%fused_computation.8 | convolution fusion | flops 8461910016 | bytes 36569088 | tf_op jit(solution)/shard_map/dot_general | solution.py:61
  251.7 16.4 %fusion.19 = (f32[672,4096]{1,0:T(8,128)}, f32[672,4096]{1,0:T(8,128)}) fusion(f32[1344,4096]{1,0:T(8,128)} %fusion.2), kind=kLoop, calls=%fused_computation.49 | loop fusion | bytes 44040192 | tf_op jit(solution)/shard_map/slice | solution.py:65
  268.1 9.1 %squeeze.19 = f32[32,21,4096]{2,1,0:T(8,128)} reshape(f32[672,4096]{1,0:T(8,128)} %get-tuple-element.5) | data formatting | bytes 22020096 | tf_op jit(solution)/shard_map/squeeze | solution.py:65
  277.2 15.0 %copy.20 = f32[32,21,4096]{2,0,1:T(8,128)} copy(f32[32,21,4096]{2,1,0:T(8,128)} %squeeze.19) | data formatting | bytes 22020096 | tf_op jit(solution)/shard_map/squeeze | solution.py:65
  292.2 0.1 collective-permute-start.1
  292.3 9.0 %squeeze.18 = f32[32,21,4096]{2,1,0:T(8,128)} reshape(f32[672,4096]{1,0:T(8,128)} %get-tuple-element.6) | data formatting | bytes 22020096 | tf_op jit(solution)/shard_map/squeeze | solution.py:65
  301.3 8.1 %collective-permute-done.1 = f32[32,21,4096]{2,0,1:T(8,128)} collective-permute-done((f32[32,21,4096]{2,0,1:T(8,128)}, f32[32,21,4096]{2,0,1:T(8,128)}, u32[]{:S(2)}, u32[]{:S(2)}) %collective-permute-start.1) | collective-permute-done | bytes 11010080 | tf_op jit(solution)/shard_map/ppermute | solution.py:16
  309.4 15.2 %fusion = bf16[32,21,4096]{2,1,0:T(8,128)(2,1)} fusion(f32[32,21,4096]{2,1,0:T(8,128)} %squeeze.18, f32[32,21,4096]{2,0,1:T(8,128)} %collective-permute-done.1), kind=kLoop, calls=%fused_computation.5 | loop fusion | flops 5505024 | bytes 27525120 | tf_op jit(solution)/shard_map/convert_element_type | solution.py:66
  324.6 4.0 all-to-all-start.1
  328.6 0.1 copy.13
  328.7 139.8 %all-to-all-done.1 = bf16[32,21,4096]{2,1,0:T(8,128)(2,1)} async-done(((bf16[32,21,4096]{2,1,0:T(8,128)(2,1)}), bf16[32,21,4096]{2,1,0:T(8,128)(2,1)}, u32[]{:S(2)}, u32[]{:S(2)}) %all-to-all-start.1) | async-done | bytes 5505056 | tf_op jit(solution)/shard_map/all_to_all | solution.py:67
  468.5 6.3 %reshape.199 = bf16[672,4096]{1,0:T(8,128)(2,1)} reshape(bf16[32,21,4096]{2,1,0:T(8,128)(2,1)} %all-to-all-done.1) | data formatting | bytes 11010048 | tf_op jit(solution)/shard_map/reshape | solution.py:69
  474.8 12.0 %gather_fusion = bf16[512,4096]{1,0:T(8,128)(2,1)} fusion(bf16[672,4096]{1,0:T(8,128)(2,1)} %reshape.199, s32[1024]{0:T(1024)S(1)} %pad_clamp_fusion), kind=kCustom, calls=%fused_computation.1 | custom fusion | bytes 8390656 | tf_op jit(solution)/shard_map/gather | solution.py:70
  486.8 6.5 %fusion.1 = bf16[64,4096]{1,0:T(8,128)(2,1)} fusion(bf16[512,4096]{1,0:T(8,128)(2,1)} %gather_fusion, f32[64,8]{1,0:T(8,128)S(1)} %copy.13), kind=kLoop, calls=%fused_computation.7 | loop fusion | flops 6029312 | bytes 4720640 | tf_op jit(solution)/shard_map/reduce_sum | solution.py:71
  (24 shorter events, 0.3 us)
Async XLA Ops:
  0.0 3.5 copy-start
  182.5 9.1 %collective-permute-start = (bf16[32,21,4096]{2,0,1:T(8,128)(2,1)S(1)}, bf16[32,21,4096]{2,0,1:T(8,128)(2,1)S(1)}, u32[]{:S(2)}, u32[]{:S(2)}) collective-permute-start(bf16[32,21,4096]{2,0,1:T(8,128)(2,1)S(1)} %copy.18), channel_id=1, source_target_pairs={{0,1},{1,0},{2,3},{3,2},{4,5},{5,4},{6,7},{7,6},{8,9},{9,8},{10,11... | collective-permute-start | bytes 16515080 | tf_op jit(solution)/shard_map/ppermute | solution.py:16
  212.7 12.8 %copy-start.2 = (bf16[1344,4096]{1,0:T(8,128)(2,1)S(1)}, bf16[1344,4096]{1,0:T(8,128)(2,1)}, u32[]{:S(2)}) copy-start(bf16[1344,4096]{1,0:T(8,128)(2,1)} %reshape.198) | copy-start | bytes 33030148
  212.7 26.7 %slice-start = ((s8[6291456]{0:T(1024)(128)(4,1)}), s8[4194304]{0:T(1024)(128)(4,1)S(1)}, s32[]{:S(2)}) async-start(s8[6291456]{0:T(1024)(128)(4,1)} %bitcast.40), calls=%async_computation.2 | async-start | bytes 8388608
  225.5 13.9 %slice-start.1 = ((s8[6291456]{0:T(1024)(128)(4,1)}), s8[2097152]{0:T(1024)(128)(4,1)S(1)}, s32[]{:S(2)}) async-start(s8[6291456]{0:T(1024)(128)(4,1)} %bitcast.40), calls=%async_computation.3 | async-start | bytes 4194304
  292.2 17.2 %collective-permute-start.1 = (f32[32,21,4096]{2,0,1:T(8,128)}, f32[32,21,4096]{2,0,1:T(8,128)}, u32[]{:S(2)}, u32[]{:S(2)}) collective-permute-start(f32[32,21,4096]{2,0,1:T(8,128)} %copy.20), channel_id=1, source_target_pairs={{0,1},{1,0},{2,3},{3,2},{4,5},{5,4},{6,7},{7,6},{8,9},{9,8},{10,11... | collective-permute-start | bytes 33030152 | tf_op jit(solution)/shard_map/ppermute | solution.py:16
  324.6 4.0 copy-start.3
  324.6 143.9 %all-to-all-start.1 = ((bf16[32,21,4096]{2,1,0:T(8,128)(2,1)}), bf16[32,21,4096]{2,1,0:T(8,128)(2,1)}, u32[]{:S(2)}, u32[]{:S(2)}) async-start(bf16[32,21,4096]{2,1,0:T(8,128)(2,1)} %fusion), calls=%async_computation.1 | async-start | bytes 12582912 | tf_op jit(solution)/shard_map/all_to_all | solution.py:67
  474.8 18.5 %copy-start.1 = (bf16[64,4096]{1,0:T(8,128)(2,1)S(1)}, bf16[64,4096]{1,0:T(8,128)(2,1)}, u32[]{:S(2)}) copy-start(bf16[64,4096]{1,0:T(8,128)(2,1)} %param.6) | copy-start | bytes 1572868
where the time goes:
time: 503 us; the launch traced here: 494 us
  waiting for transfers between devices  157 us (31%)
  blocking collectives  148 us (29%)
  local copies, waits for them, and re-layouts  116 us (23%)
  matrix products  38.9 us (8%)
  other arithmetic  29.6 us (6%)
    all_to_all x1, blocking collectives, on_device(): lax.all_to_all(outgoing.reshape(devices_all, per_half, width), ('dp', 'ex...  148 us
    all_to_all x1, waiting for transfers between devices, on_device(): lax.all_to_all(results, ('dp', 'expert'), split_axis=0, concat_axis=0, ti...  140 us
    squeeze x3, local copies, waits for them, and re-layouts, on_device(): total = partial_out[0] + from_partner(partial_out[1], 'expert', 0)  33.1 us
    scatter x1, local copies, waits for them, and re-layouts, on_device(): jnp.zeros((devices_all * per_half, width), jnp.bfloat16).at[place]  21.8 us
    ppermute x2, waiting for transfers between devices, from_partner(): return lax.ppermute(block, axis, route)  17.1 us
    slice x1, local copies, waits for them, and re-layouts, on_device(): total = partial_out[0] + from_partner(partial_out[1], 'expert', 0)  16.4 us
    convert_element_type x1, other arithmetic, on_device(): results = total.astype(jnp.bfloat16)  15.2 us
    dot_general x1, matrix products, half_hidden(): gate = jnp.dot(rows, gate_part, preferred_element_type=jnp.float32)  13.8 us
  transfers between devices with their start and end apart: 3, of which 3 were waited for; matrix products, arithmetic and copies ran while one was open for 2% of the time, Pallas kernels for 0%

commit v1 on v0

v1 whole, which is shorter than its diff:
```python
import functools

import jax
import jax.numpy as jnp
from jax import lax
from jax.experimental import pallas as pl
from jax.experimental.pallas import tpu as pltpu
from jax.sharding import PartitionSpec as P

TOP = 8
FOLD = 8
SUB = 16
TILE = 256
F32 = jnp.float32
BF16 = jnp.bfloat16
VMEM = pl.BlockSpec(memory_space=pltpu.VMEM)
SMEM = pl.BlockSpec(memory_space=pltpu.SMEM)
ANY = pl.BlockSpec(memory_space=pl.ANY)


def iota(shape, dim):
    return lax.broadcasted_iota(jnp.int32, shape, dim)


def heights(cap):
    main = cap // SUB * SUB
    tail = cap - main
    return main, tail, main + (SUB if tail else 0)


def unfold(block, cap, rows_ref, base):
    main, tail, high = heights(cap)
    part = block.shape[1]
    if tail:
        shape = (FOLD * SUB, FOLD * tail)
        r, c = iota(shape, 0), iota(shape, 1)
        spread = ((r % SUB < tail) & (c == r // SUB * tail + r % SUB)).astype(BF16)
        last = jnp.dot(spread, block[FOLD * main :, :], preferred_element_type=F32).astype(BF16)
    for g in range(FOLD):
        cols = slice(g * part, (g + 1) * part)
        if main:
            rows_ref[base : base + main, cols] = block[g * main : (g + 1) * main, :]
        if tail:
            rows_ref[base + main : base + high, cols] = last[g * SUB : (g + 1) * SUB]


def fold(rows_ref, base, cap, block):
    main, tail, high = heights(cap)
    part = block.shape[1]
    columns = [slice(g * part, (g + 1) * part) for g in range(FOLD)]
    if main:
        for g, cols in enumerate(columns):
            block[g * main : (g + 1) * main, :] = rows_ref[base : base + main, cols]
    if tail:
        last = jnp.concatenate([rows_ref[base + main : base + high, cols] for cols in columns], axis=0)
        shape = (FOLD * tail, FOLD * SUB)
        r, c = iota(shape, 0), iota(shape, 1)
        gather = ((c % SUB < tail) & (r == c // SUB * tail + c % SUB)).astype(BF16)
        block[FOLD * main :, :] = jnp.dot(gather, last, preferred_element_type=F32).astype(BF16)


def slot_codes(weights):
    rows = weights.shape[0]
    named = weights > 0.0
    tri = (iota((rows, rows), 0) > iota((rows, rows), 1)).astype(BF16)
    slots = jnp.dot(tri, named.astype(BF16), preferred_element_type=F32)
    return jnp.where(named, slots, -1.0)


def column(values, which):
    return jnp.sum(jnp.where(iota(values.shape, 1) == which, values, 0.0), axis=1, keepdims=True)


def pack_body(cap, ids_ref, x_ref, weights, outs, rows_ref):
    tokens = x_ref.shape[0]
    high = heights(cap)[2]
    codes = slot_codes(weights)
    square = (tokens, tokens)
    picks = []
    for m in range(len(outs)):
        col = column(codes, ids_ref[m])
        row = jnp.sum(
            jnp.where(iota(square, 0) == iota(square, 1), col, 0.0), axis=0, keepdims=True
        ).astype(jnp.int32)
        picks.append((iota((high, tokens), 0) == row).astype(BF16))
    pick = jnp.concatenate(picks, axis=0)
    rows_ref[...] = jnp.dot(pick, x_ref[...], preferred_element_type=F32).astype(BF16)
    for m, out in enumerate(outs):
        fold(rows_ref, m * high, cap, out)


def tie(value, *others):
    return lax.optimization_barrier((value, *others))[0]


def tail_width(expert_count):
    return -(-3 * expert_count // 128) * 128


def first_kernel(n, cap, ids_ref, x_ref, routes_ref, gate_ref, *refs):
    w_ref, wide_ref, outs, rows_ref = refs[0], refs[1], refs[2 : 2 + n], refs[2 + n]
    quant = gate_ref[...].astype(F32)
    chosen = quant / jnp.sum(quant, axis=1, keepdims=True)
    routes = routes_ref[...]
    experts = iota(w_ref.shape, 1)
    weights = jnp.zeros(w_ref.shape, F32)
    for k in range(TOP):
        weights += jnp.where(experts == routes[:, k : k + 1], chosen[:, k : k + 1], 0.0)
    w_ref[...] = weights
    width, count = x_ref.shape[1], w_ref.shape[1]
    wide_ref[:, :width] = x_ref[...]
    terms, rest = [], weights
    for _ in range(3):
        terms.append(rest.astype(BF16))
        rest = rest - terms[-1].astype(F32)
    fill = wide_ref.shape[1] - width - 3 * count
    terms.append(jnp.zeros((w_ref.shape[0], fill), BF16))
    wide_ref[:, width:] = jnp.concatenate(terms, axis=1)
    pack_body(cap, ids_ref, x_ref, weights, outs, rows_ref)


def first(x, routes, gate_fixed, ids, cap, expert_count):
    rows, width = x.shape
    n = ids.shape[0]
    shape = jax.ShapeDtypeStruct((cap * FOLD, width // FOLD), x.dtype)
    return pl.pallas_call(
        functools.partial(first_kernel, n, cap),
        out_shape=(
            jax.ShapeDtypeStruct((rows, expert_count), F32),
            jax.ShapeDtypeStruct((rows, width + tail_width(expert_count)), BF16),
        )
        + (shape,) * n,
        in_specs=[SMEM, VMEM, VMEM, VMEM],
        out_specs=(VMEM,) * (2 + n),
        scratch_shapes=[pltpu.VMEM((n * heights(cap)[2], width), BF16)],
        compiler_params=pltpu.CompilerParams(vmem_limit_bytes=12 << 20),
        name="first",
    )(ids, x, routes, gate_fixed)


def pack_kernel(n, cap, ids_ref, wide_ref, *refs):
    w_ref, outs, rows_ref = refs[-2 - n], refs[-1 - n : -1], refs[-1]
    width, count = rows_ref.shape[1], w_ref.shape[1]
    shape = (wide_ref.shape[1] - width, count)
    r, c = iota(shape, 0), iota(shape, 1)
    add = ((r == c) | (r == c + count) | (r == c + 2 * count)).astype(BF16)
    weights = jnp.dot(wide_ref[:, width:], add, preferred_element_type=F32)
    w_ref[...] = weights
    pack_body(cap, ids_ref, wide_ref.at[:, :width], weights, outs, rows_ref)


def pack(wide, ids, cap, expert_count, after=()):
    rows = wide.shape[0]
    width = wide.shape[1] - tail_width(expert_count)
    n = ids.shape[0]
    shape = jax.ShapeDtypeStruct((cap * FOLD, width // FOLD), wide.dtype)
    return pl.pallas_call(
        functools.partial(pack_kernel, n, cap),
        out_shape=(jax.ShapeDtypeStruct((rows, expert_count), F32),) + (shape,) * n,
        in_specs=[SMEM, VMEM] + [ANY] * len(after),
        out_specs=(VMEM,) * (1 + n),
        scratch_shapes=[pltpu.VMEM((n * heights(cap)[2], width), BF16)],
        compiler_params=pltpu.CompilerParams(vmem_limit_bytes=12 << 20),
        name="pack",
    )(ids, wide, *after)


def expert_body(n, cap, blocks, weights, outs, x_ref, h_ref, y_ref, ready):
    high = heights(cap)[2]
    half, width = weights[2].shape[1:]
    for m in range(n):
        unfold(blocks[m], cap, x_ref, m * high)
    x = x_ref[...]
    steps = expert_steps(half, width)
    for i, (s, j) in enumerate(steps):
        ready(i)
        if s is not None:
            g, u = weights[3 * s : 3 * s + 2]
            gate = jnp.dot(x, g[0, :, j : j + TILE], preferred_element_type=F32)
            upper = jnp.dot(x, u[0, :, j : j + TILE], preferred_element_type=F32)
            hidden = gate / (1.0 + jnp.exp(-gate)) * upper
            h_ref[:, s * half + j : s * half + j + TILE] = hidden.astype(BF16)
        else:
            total = sum(
                jnp.dot(
                    h_ref[:, t * half : (t + 1) * half],
                    weights[3 * t + 2][0, :, j : j + 2 * TILE],
                    preferred_element_type=F32,
                )
                for t in range(2)
            )
            y_ref[:, j : j + 2 * TILE] = total.astype(BF16)
    for m in range(n):
        fold(y_ref, m * high, cap, outs[m])


def expert_steps(half, width):
    hidden = [(s, j) for s in range(2) for j in range(0, half, TILE)]
    return hidden + [(None, j) for j in range(0, width, 2 * TILE)]


def expert_kernel(n, cap, *refs):
    blocks, weights = refs[:n], refs[n : n + 6]
    outs, scratch = refs[-3 - n : -3], refs[-3:]
    expert_body(n, cap, blocks, weights, outs, *scratch, lambda i: None)


def expert_first_kernel(n, cap, *refs):
    blocks, sources = refs[:n], refs[n : n + 6]
    refs = refs[-4 - n - 6 :]
    outs, weights, scratch, sems = refs[:n], refs[n : n + 6], refs[n + 6 : -1], refs[-1]
    half, width = weights[2].shape[1:]
    steps = expert_steps(half, width)
    depth = sems.shape[0]

    def copies(i):
        s, j = steps[i]
        if s is not None:
            which, cols = (3 * s, 3 * s + 1), pl.ds(j, TILE)
        else:
            which, cols = (2, 5), pl.ds(j, 2 * TILE)
        return [
            pltpu.make_async_copy(
                sources[w].at[0, :, cols], weights[w].at[0, :, cols], sems.at[i % depth, t]
            )
            for t, w in enumerate(which)
        ]

    def ready(i):
        for copy in copies(i):
            copy.wait()
        if i + depth < len(steps):
            for copy in copies(i + depth):
                copy.start()

    for i in range(depth):
        for copy in copies(i):
            copy.start()
    expert_body(n, cap, blocks, weights, outs, *scratch, ready)


def expert(blocks, weights, cap, after=(), first_call=False):
    n = len(blocks)
    half, width = weights[2].shape[1:]
    rows = n * heights(cap)[2]
    out_shape = tuple(jax.ShapeDtypeStruct(b.shape, b.dtype) for b in blocks)
    scratch = [
        pltpu.VMEM((rows, width), BF16),
        pltpu.VMEM((rows, 2 * half), BF16),
        pltpu.VMEM((rows, width), BF16),
    ]
    if first_call:
        kernel, space, name = expert_first_kernel, ANY, "expert_first"
        out_shape += tuple(pltpu.VMEM(w.shape, w.dtype) for w in weights)
        scratch.append(pltpu.SemaphoreType.DMA((3, 2)))
    else:
        kernel, space, name = expert_kernel, VMEM, "expert"
        weights = [pltpu.with_memory_space_constraint(w, pltpu.VMEM) for w in weights]
    result = pl.pallas_call(
        functools.partial(kernel, n, cap),
        out_shape=out_shape,
        in_specs=[VMEM] * n + [space] * 6 + [ANY] * len(after),
        out_specs=(VMEM,) * len(out_shape),
        scratch_shapes=scratch,
        compiler_params=pltpu.CompilerParams(vmem_limit_bytes=18 << 20),
        name=name,
    )(*blocks, *weights, *after)
    return list(result[:n]), list(result[n:])


def combine_kernel(n, n_others, cap, ids_ref, w_ref, *refs):
    blocks, others = refs[:n], refs[n : n + n_others]
    out_ref, rows_ref = refs[-2:]
    tokens = out_ref.shape[0]
    high = heights(cap)[2]
    weights = w_ref[...]
    codes = slot_codes(weights)
    total = None
    for m in range(n):
        unfold(blocks[m], cap, rows_ref, m * high)
        code = column(codes, ids_ref[m]).astype(jnp.int32)
        pick = (code == iota((tokens, high), 1)).astype(BF16)
        rows = jnp.dot(pick, rows_ref[m * high : (m + 1) * high, :], preferred_element_type=F32)
        term = column(weights, ids_ref[m]) * rows
        total = term if total is None else total + term
    for other in others:
        total += other[...].astype(F32)
    out_ref[...] = total.astype(BF16)


def combine(blocks, weights, ids, cap, others=(), after=()):
    n = len(blocks)
    width = blocks[0].shape[1] * FOLD
    return pl.pallas_call(
        functools.partial(combine_kernel, n, len(others), cap),
        out_shape=jax.ShapeDtypeStruct((weights.shape[0], width), BF16),
        in_specs=[SMEM] + [VMEM] * (1 + n + len(others)) + [ANY] * len(after),
        out_specs=VMEM,
        scratch_shapes=[pltpu.VMEM((n * heights(cap)[2], width), BF16)],
        compiler_params=pltpu.CompilerParams(vmem_limit_bytes=12 << 20),
        name="combine",
    )(ids, weights, *blocks, *others, *after)


def on_device(tokens, routes, gate_fixed, w_gate, w_up, w_down):
    n_data = lax.axis_size("dp")
    n_owner = lax.axis_size("expert")
    line = n_owner // 2
    expert_count = n_data * line
    cap = 2 * (5 * tokens.shape[0] * TOP // (8 * expert_count) + 1)
    dp = lax.axis_index("dp")
    z = lax.axis_index("expert") // 2
    ids = jnp.stack([(dp ^ m) * line + z for m in range(n_data)]).astype(jnp.int32)

    def along(block, step):
        pairs = [(i, (i + 2 * step) % n_owner) for i in range(n_owner)]
        return lax.ppermute(block, "expert", pairs)

    def across(block, m):
        return lax.ppermute(block, "dp", [(i, i ^ m) for i in range(n_data)])

    def swap(block):
        return lax.ppermute(block, "expert", [(i, i ^ 1) for i in range(n_owner)])

    last = n_data - 1

    def exchange(lists, after=None):
        got = [lists[0]] + [across(lists[m], m) for m in range(1, last)]
        if last:
            got.append(across(tie(lists[last], *got[1:2]), last))
        return got

    weights, wide, *lists = first(tokens, routes, gate_fixed, ids, cap, expert_count)
    other = [swap(w_gate), swap(w_up)]
    ws, sent = [weights], [exchange(lists)]
    after = (*sent[0][1:last], *other)
    for k in range(1, line):
        wide = along(wide, 1)
        weights, *lists = pack(wide, ids, cap, expert_count, after=after)
        ws.append(weights)
        sent.append(exchange(lists))
        after = (*sent[k - 1][last:], *sent[k][1:last])
        if k == 1:
            other.append(swap(tie(w_down, lists[0])))
            after += (other[2],)
        if k == 2:
            held = [w_gate, w_up, w_down, *other]
            outs, held = expert(sent[0], held, cap, after=(lists[0],), first_call=True)
            result = {0: outs}
            after += (outs[0],)

    after = lists[:1]
    order = list(range(1, line))
    back = {}

    def send_back(k, after):
        part = combine(result[k], ws[k], ids, cap, after=after)
        back[k] = along(part, -k)
        return [part]

    for i, k in enumerate(order):
        if i >= 2:
            after = send_back(order[i - 2], after)
        outs, _ = expert(sent[k], held, cap, after=after)
        after = outs[:1]
        result[k] = [outs[0]] + [across(outs[m], m) for m in range(1, n_data)]
    result[0] = [result[0][0]] + [across(tie(result[0][m], after[0]), m) for m in range(1, n_data)]
    for k in order:
        if k not in back:
            send_back(k, after)
    return combine(result[0], ws[0], ids, cap, others=list(back.values()))


def solution(mesh):
    placed = (
        P(("dp", "expert"), None),
        P(("dp", "expert"), None),
        P(("dp", "expert"), None),
        P(("dp", "expert"), None, None),
        P(("dp", "expert"), None, None),
        P(("dp", "expert"), None, None),
    )
    return jax.shard_map(
        on_device, mesh=mesh, in_specs=placed, out_specs=P(("dp", "expert"), None), check_vma=False
    )
```

time: 503 us -> 177 us (0.35); the launches traced: 494 us -> 177 us
  blocking collectives: 148 us -> 0 us
  local copies, waits for them, and re-layouts: 116 us -> 9.76 us
  waiting for transfers between devices: 157 us -> 67.3 us
  Pallas kernels: 0 us -> 63.3 us
  matrix products: 38.9 us -> 0 us
  starting transfers between devices: 4.15 us -> 35.8 us
  other arithmetic: 29.6 us -> 0.08 us
    all_to_all x1 -> x0, blocking collectives: 148 us -> none  [on_device(): lax.all_to_all(outgoing.reshape(devices_all, per_half, width), ('dp', 'ex...]
    all_to_all x1 -> x0, waiting for transfers between devices: 140 us -> none  [on_device(): lax.all_to_all(results, ('dp', 'expert'), split_axis=0, concat_axis=0, ti...]
    pallas_call x0 -> x12, Pallas kernels: none -> 63.3 us  [the longest x4 47 us: expert(): pl.pallas_call(functools.partial(kernel, n, cap), out_shape=out_shape, in...]
    ppermute x2 -> x33, waiting for transfers between devices: 17.1 us -> 67.3 us  [the longest x24 48.3 us: across(): return lax.ppermute(block, 'dp', [(i, i ^ m) for i in range(n_data)])]
    dot_general x3 -> x0, matrix products: 38.9 us -> none  [the longest x1 13.8 us: half_hidden(): gate = jnp.dot(rows, gate_part, preferred_element_type=jnp.float32)]
    ppermute x2 -> x33, starting transfers between devices: 0.2 us -> 35.8 us  [the longest x24 28.4 us: across(): return lax.ppermute(block, 'dp', [(i, i ^ m) for i in range(n_data)])]
    squeeze x3 -> x0, local copies, waits for them, and re-layouts: 33.1 us -> none  [on_device(): total = partial_out[0] + from_partner(partial_out[1], 'expert', 0)]
    reshape x3 -> x0, local copies, waits for them, and re-layouts: 24.7 us -> none  [the longest x1 12.1 us: on_device(): rows = jnp.concatenate([arrived, partner], axis=0).reshape(-1, width)]
  transfers between devices with their start and end apart: 3 -> 33, of which waited for: 3 -> 15; matrix products, arithmetic and copies ran while one was open for 2% -> 1% of each run, Pallas kernels for 0% -> 32%
where the time goes in v1:
time: 177 us
  waiting for transfers between devices  67.3 us (38%)
  Pallas kernels  63.3 us (36%)
  starting transfers between devices  35.8 us (20%)
  local copies, waits for them, and re-layouts  9.76 us (6%)
    ppermute x24, waiting for transfers between devices, across(): return lax.ppermute(block, 'dp', [(i, i ^ m) for i in range(n_data)])  48.3 us
    pallas_call x4, Pallas kernels, expert(): pl.pallas_call(functools.partial(kernel, n, cap), out_shape=out_shape, in...  47 us
    ppermute x24, starting transfers between devices, across(): return lax.ppermute(block, 'dp', [(i, i ^ m) for i in range(n_data)])  28.4 us
    ppermute x6, waiting for transfers between devices, along(): return lax.ppermute(block, 'expert', pairs)  19 us
    unnamed x64, local copies, waits for them, and re-layouts  9.76 us
    pallas_call x4, Pallas kernels, combine(): pl.pallas_call(functools.partial(combine_kernel, n, len(others), cap), ou...  8.34 us
    ppermute x6, starting transfers between devices, along(): return lax.ppermute(block, 'expert', pairs)  6.75 us
    pallas_call x3, Pallas kernels, pack(): pl.pallas_call(functools.partial(pack_kernel, n, cap), out_shape=(jax.Sha...  6.19 us
  transfers between devices with their start and end apart: 33, of which 15 were waited for; matrix products, arithmetic and copies ran while one was open for 1% of the time, Pallas kernels for 32%

profile of v1, /device:TPU:0, one launch (start us, length us, event | category | flops | bytes accessed | tf_op | source)
XLA Modules:
  0.0 176.5 jit_solution(14517802461454746581)
XLA Ops:
  3.2 1.8 %first.1 = (f32[64,16]{1,0:T(8,128)S(1)}, bf16[64,4224]{1,0:T(8,128)(2,1)S(1)}, bf16[336,512]{1,0:T(8,128)(2,1)S(1)}, bf16[336,512]{1,0:T(8,128)(2,1)S(1)}, bf16...) custom-call(s32[4]{0:T(128)S(1)} %pad_add_fusion.ids_ref, bf16[64,4096]{1,0:T(8,128)(2,1)S(1)} %copy-done.19, ...), custom_call_target="tpu_custom_call" | custom-call | tf_op jit(solution)/shard_map/first/pallas_call | solution.py:126
  5.7 3.0 %collective-permute-start.5 = (bf16[64,4224]{1,0:T(8,128)(2,1)S(1)}, bf16[64,4224]{1,0:T(8,128)(2,1)S(1)}, u32[]{:S(2)}, u32[]{:S(2)}) collective-permute-start(bf16[64,4224]{1,0:T(8,128)(2,1)S(1)} %get-tuple-element.62), channel_id=1, source_target_pairs={{0,2},{1,3},{2,4},{3,5},{4,6},{5,7},{6,0},{7,1},{8,10},{9,11},{10,... | collective-permute-start | bytes 1622024 | tf_op jit(solution)/shard_map/ppermute | solution.py:317
  8.8 1.5 collective-permute-start
  10.3 1.5 collective-permute-start.1
  11.8 6.7 %collective-permute-done.refs_0_.refs_1_ = bf16[336,512]{1,0:T(8,128)(2,1)S(1)} collective-permute-done((bf16[336,512]{1,0:T(8,128)(2,1)S(1)}, bf16[336,512]{1,0:T(8,128)(2,1)S(1)}, u32[]{:S(2)}, u32[]{:S(2)}) %collective-permute-start) | collective-permute-done | bytes 344096 | tf_op jit(solution)/shard_map/ppermute | solution.py:320
  19.7 3.6 %collective-permute-done.5.wide_ref = bf16[64,4224]{1,0:T(8,128)(2,1)S(1)} collective-permute-done((bf16[64,4224]{1,0:T(8,128)(2,1)S(1)}, bf16[64,4224]{1,0:T(8,128)(2,1)S(1)}, u32[]{:S(2)}, u32[]{:S(2)}) %collective-permute-start.5) | collective-permute-done | bytes 540704 | tf_op jit(solution)/shard_map/ppermute | solution.py:317
  23.2 1.6 pack.3
  25.1 2.5 %collective-permute-start.2 = (bf16[336,512]{1,0:T(8,128)(2,1)S(1)}, bf16[336,512]{1,0:T(8,128)(2,1)S(1)}, u32[]{:S(2)}, u32[]{:S(2)}) collective-permute-start(bf16[336,512]{1,0:T(8,128)(2,1)S(1)} %get-tuple-element.61), channel_id=1, source_target_pairs={{0,24},{8,16},{16,8},{24,0},{1,25},{9,17},{17,9},{25,1},{2,26},{10... | collective-permute-start | bytes 1032200 | tf_op jit(solution)/shard_map/ppermute | solution.py:320
  28.6 12.8 %collective-permute-done.7.wide_ref = bf16[64,4224]{1,0:T(8,128)(2,1)S(1)} collective-permute-done((bf16[64,4224]{1,0:T(8,128)(2,1)S(1)}, bf16[64,4224]{1,0:T(8,128)(2,1)S(1)}, u32[]{:S(2)}, u32[]{:S(2)}) %collective-permute-start.7) | collective-permute-done | bytes 540704 | tf_op jit(solution)/shard_map/ppermute | solution.py:317
  41.5 2.4 %collective-permute-done.8.refs_1_ = bf16[336,512]{1,0:T(8,128)(2,1)S(1)} collective-permute-done((bf16[336,512]{1,0:T(8,128)(2,1)S(1)}, bf16[336,512]{1,0:T(8,128)(2,1)S(1)}, u32[]{:S(2)}, u32[]{:S(2)}) %collective-permute-start.8) | collective-permute-done | bytes 344096 | tf_op jit(solution)/shard_map/ppermute | solution.py:320
  43.9 2.9 %pack.4 = (f32[64,16]{1,0:T(8,128)S(1)}, bf16[336,512]{1,0:T(8,128)(2,1)S(1)}, bf16[336,512]{1,0:T(8,128)(2,1)}, bf16[336,512]{1,0:T(8,128)(2,1)}, bf16[336,512]{1,0:T(8,128)(2,1)S(1)}) custom-call(s32[4]{0:T(128)S(1)} %pad_add_fusion.ids_ref, bf16[64,4224]{1,0:T(8,128)(2,1)S(1)} %collective-permute-done.7.wide_ref, ...), custom_call_target="tpu_custom_call" | custom-call | tf_op jit(solution)/shard_map/pack/pallas_call | solution.py:157
  51.0 16.3 %expert_first.1 = (bf16[336,512]{1,0:T(8,128)(2,1)}, bf16[336,512]{1,0:T(8,128)(2,1)}, bf16[336,512]{1,0:T(8,128)(2,1)}, bf16[336,512]{1,0:T(8,128)(2,1)}, bf16[...) custom-call(bf16[336,512]{1,0:T(8,128)(2,1)} %copy-done.21, ...), custom_call_target="tpu_custom_call" | custom-call | tf_op jit(solution)/shard_map/expert_first/pallas_call | solution.py:259
  68.6 1.6 pack.5
  73.8 10.4 %expert.3 = (bf16[336,512]{1,0:T(8,128)(2,1)}, bf16[336,512]{1,0:T(8,128)(2,1)}, bf16[336,512]{1,0:T(8,128)(2,1)}, bf16[336,512]{1,0:T(8,128)(2,1)}) custom-call(bf16[336,512]{1,0:T(8,128)(2,1)} %copy-done.20, bf16[336,512]{1,0:T(8,128)(2,1)} %copy-done.10, bf16[336,512]{1,0:T(8,128)(2,1)} %copy-done.11, bf16[336,512]{1,0:T(8,128)(2,1)} %copy-done.16, ...), custom_call_target="tpu_custom_call" | custom-call | tf_op jit(solution)/shard_map/expert/pallas_call | solution.py:259
  84.2 1.5 collective-permute-start.17
  88.4 1.7 collective-permute-done.20.refs_3_
  91.4 10.2 %expert.4 = (bf16[336,512]{1,0:T(8,128)(2,1)}, bf16[336,512]{1,0:T(8,128)(2,1)}, bf16[336,512]{1,0:T(8,128)(2,1)}, bf16[336,512]{1,0:T(8,128)(2,1)}) custom-call(bf16[336,512]{1,0:T(8,128)(2,1)} %copy-done.18, bf16[336,512]{1,0:T(8,128)(2,1)} %copy-done.14, bf16[336,512]{1,0:T(8,128)(2,1)} %copy-done.15, bf16[336,512]{1,0:T(8,128)(2,1)} %copy-done.25, ...), custom_call_target="tpu_custom_call" | custom-call | tf_op jit(solution)/shard_map/expert/pallas_call | solution.py:259
  102.7 9.1 %collective-permute-done.18.refs_2_ = bf16[336,512]{1,0:T(8,128)(2,1)S(1)} collective-permute-done((bf16[336,512]{1,0:T(8,128)(2,1)}, bf16[336,512]{1,0:T(8,128)(2,1)S(1)}, u32[]{:S(2)}, u32[]{:S(2)}) %collective-permute-start.18) | collective-permute-done | bytes 344096 | tf_op jit(solution)/shard_map/ppermute | solution.py:320
  114.7 1.8 %combine.4.refs_10_ = bf16[64,4096]{1,0:T(8,128)(2,1)S(1)} custom-call(s32[4]{0:T(128)S(1)} %pad_add_fusion.ids_ref, f32[64,16]{1,0:T(8,128)S(1)} %get-tuple-element.85.w_ref, bf16[336,512]{1,0:T(8,128)(2,1)S(1)} %copy-done.13, bf16[336,512]{1,0:T(8,128)(2,1)S(1)} %collective-permute-done.17.refs_1_, bf16[336,512]{1,0:T(8,128)(2,1)S(1)} %collective-permute-done.18.refs_2_, ...), custom_call_target="tpu_custom_call" | custom-call | tf_op jit(solution)/shard_map/combine/pallas_call | solution.py:294
  116.6 10.2 %collective-permute-done.15.refs_2_ = bf16[336,512]{1,0:T(8,128)(2,1)S(1)} collective-permute-done((bf16[336,512]{1,0:T(8,128)(2,1)S(1)}, bf16[336,512]{1,0:T(8,128)(2,1)S(1)}, u32[]{:S(2)}, u32[]{:S(2)}) %collective-permute-start.15) | collective-permute-done | bytes 344096 | tf_op jit(solution)/shard_map/ppermute | solution.py:320
  126.8 3.5 %collective-permute-start.24 = (bf16[64,4096]{1,0:T(8,128)(2,1)S(1)}, bf16[64,4096]{1,0:T(8,128)(2,1)S(1)}, u32[]{:S(2)}, u32[]{:S(2)}) collective-permute-start(bf16[64,4096]{1,0:T(8,128)(2,1)S(1)} %combine.4.refs_10_), channel_id=1, source_target_pairs={{0,6},{1,7},{2,0},{3,1},{4,2},{5,3},{6,4},{7,5},{8,14},{9,15},{10,... | collective-permute-start | bytes 1572872 | tf_op jit(solution)/shard_map/ppermute | solution.py:317
  131.1 10.1 %expert.5 = (bf16[336,512]{1,0:T(8,128)(2,1)}, bf16[336,512]{1,0:T(8,128)(2,1)}, bf16[336,512]{1,0:T(8,128)(2,1)}, bf16[336,512]{1,0:T(8,128)(2,1)}) custom-call(bf16[336,512]{1,0:T(8,128)(2,1)} %copy-done.17, bf16[336,512]{1,0:T(8,128)(2,1)} %copy-done.22, bf16[336,512]{1,0:T(8,128)(2,1)} %copy-done.23, bf16[336,512]{1,0:T(8,128)(2,1)} %copy-done.24, ...), custom_call_target="tpu_custom_call" | custom-call | tf_op jit(solution)/shard_map/expert/pallas_call | solution.py:259
  142.7 2.0 %collective-permute-start.31 = (bf16[336,512]{1,0:T(8,128)(2,1)}, bf16[336,512]{1,0:T(8,128)(2,1)S(1)}, u32[]{:S(2)}, u32[]{:S(2)}) collective-permute-start(bf16[336,512]{1,0:T(8,128)(2,1)} %get-tuple-element.106), channel_id=1, source_target_pairs={{0,24},{8,16},{16,8},{24,0},{1,25},{9,17},{17,9},{25,1},{2,26},{10... | collective-permute-start | bytes 1032200 | tf_op jit(solution)/shard_map/ppermute | solution.py:320
  145.7 1.8 %combine.5 = bf16[64,4096]{1,0:T(8,128)(2,1)S(1)} custom-call(s32[4]{0:T(128)S(1)} %pad_add_fusion.ids_ref, f32[64,16]{1,0:T(8,128)S(1)} %get-tuple-element.99.w_ref, bf16[336,512]{1,0:T(8,128)(2,1)S(1)} %copy-done.5, bf16[336,512]{1,0:T(8,128)(2,1)S(1)} %collective-permute-done.25.refs_1_, bf16[336,512]{1,0:T(8,128)(2,1)S(1)} %collective-permute-done.26.refs_2_, ...), custom_call_target="tpu_custom_call" | custom-call | tf_op jit(solution)/shard_map/combine/pallas_call | solution.py:294
  148.8 3.6 %collective-permute-done.30.refs_2_ = bf16[336,512]{1,0:T(8,128)(2,1)S(1)} collective-permute-done((bf16[336,512]{1,0:T(8,128)(2,1)}, bf16[336,512]{1,0:T(8,128)(2,1)S(1)}, u32[]{:S(2)}, u32[]{:S(2)}) %collective-permute-start.30) | collective-permute-done | bytes 344096 | tf_op jit(solution)/shard_map/ppermute | solution.py:320
  152.5 3.9 %collective-permute-done.31.refs_3_ = bf16[336,512]{1,0:T(8,128)(2,1)S(1)} collective-permute-done((bf16[336,512]{1,0:T(8,128)(2,1)}, bf16[336,512]{1,0:T(8,128)(2,1)S(1)}, u32[]{:S(2)}, u32[]{:S(2)}) %collective-permute-start.31) | collective-permute-done | bytes 344096 | tf_op jit(solution)/shard_map/ppermute | solution.py:320
  157.3 1.9 %combine.6 = bf16[64,4096]{1,0:T(8,128)(2,1)S(1)} custom-call(s32[4]{0:T(128)S(1)} %pad_add_fusion.ids_ref, f32[64,16]{1,0:T(8,128)S(1)} %get-tuple-element.103.w_ref, bf16[336,512]{1,0:T(8,128)(2,1)S(1)} %copy-done.2, bf16[336,512]{1,0:T(8,128)(2,1)S(1)} %collective-permute-done.29.refs_1_, bf16[336,512]{1,0:T(8,128)(2,1)S(1)} %collective-permute-done.30.refs_2_, ...), custom_call_target="tpu_custom_call" | custom-call | tf_op jit(solution)/shard_map/combine/pallas_call | solution.py:294
  159.9 2.3 %collective-permute-start.22 = (bf16[336,512]{1,0:T(8,128)(2,1)S(1)}, bf16[336,512]{1,0:T(8,128)(2,1)S(1)}, u32[]{:S(2)}, u32[]{:S(2)}) collective-permute-start(bf16[336,512]{1,0:T(8,128)(2,1)S(1)} %copy-done.27), channel_id=1, source_target_pairs={{0,16},{8,24},{16,0},{24,8},{1,17},{9,25},{17,1},{25,9},{2,18},{10... | collective-permute-start | bytes 1032200 | tf_op jit(solution)/shard_map/ppermute | solution.py:320
  162.8 3.8 %collective-permute-done.21.refs_1_ = bf16[336,512]{1,0:T(8,128)(2,1)S(1)} collective-permute-done((bf16[336,512]{1,0:T(8,128)(2,1)S(1)}, bf16[336,512]{1,0:T(8,128)(2,1)S(1)}, u32[]{:S(2)}, u32[]{:S(2)}) %collective-permute-start.21) | collective-permute-done | bytes 344096 | tf_op jit(solution)/shard_map/ppermute | solution.py:320
  166.6 4.1 %collective-permute-done.22.refs_2_ = bf16[336,512]{1,0:T(8,128)(2,1)S(1)} collective-permute-done((bf16[336,512]{1,0:T(8,128)(2,1)S(1)}, bf16[336,512]{1,0:T(8,128)(2,1)S(1)}, u32[]{:S(2)}, u32[]{:S(2)}) %collective-permute-start.22) | collective-permute-done | bytes 344096 | tf_op jit(solution)/shard_map/ppermute | solution.py:320
  171.2 2.6 %collective-permute-done.28.refs_5_ = bf16[64,4096]{1,0:T(8,128)(2,1)S(1)} collective-permute-done((bf16[64,4096]{1,0:T(8,128)(2,1)S(1)}, bf16[64,4096]{1,0:T(8,128)(2,1)S(1)}, u32[]{:S(2)}, u32[]{:S(2)}) %collective-permute-start.28) | collective-permute-done | bytes 524320 | tf_op jit(solution)/shard_map/ppermute | solution.py:317
  173.7 2.8 %combine.7 = bf16[64,4096]{1,0:T(8,128)(2,1)} custom-call(s32[4]{0:T(128)S(1)} %pad_add_fusion.ids_ref, f32[64,16]{1,0:T(8,128)S(1)} %get-tuple-element.56.w_ref, bf16[336,512]{1,0:T(8,128)(2,1)S(1)} %copy-done.7, bf16[336,512]{1,0:T(8,128)(2,1)S(1)} %collective-permute-done.21.refs_1_, bf16[336,512]{1,0:T(8,128)(2,1)S(1)} %collective-permute-done.22.refs_2_, ...), custom_call_target="tpu_custom_call" | custom-call | tf_op jit(solution)/shard_map/combine/pallas_call | solution.py:294
  (112 shorter events, 30.6 us)
Async XLA Ops:
  0.0 23.2 %collective-permute-start.3 = (bf16[1,4096,768]{2,1,0:T(8,128)(2,1)}, bf16[1,4096,768]{2,1,0:T(8,128)(2,1)}, u32[]{:S(2)}, u32[]{:S(2)}) collective-permute-start(bf16[1,4096,768]{2,1,0:T(8,128)(2,1)} %refs_4_.1), channel_id=1, source_target_pairs={{0,1},{1,0},{2,3},{3,2},{4,5},{5,4},{6,7},{7,6},{8,9},{9,8},{10,11... | collective-permute-start | bytes 18874376 | tf_op jit(solution)/shard_map/ppermute | solution.py:323
  0.5 22.8 %collective-permute-start.4 = (bf16[1,4096,768]{2,1,0:T(8,128)(2,1)}, bf16[1,4096,768]{2,1,0:T(8,128)(2,1)}, u32[]{:S(2)}, u32[]{:S(2)}) collective-permute-start(bf16[1,4096,768]{2,1,0:T(8,128)(2,1)} %refs_5_.1), channel_id=1, source_target_pairs={{0,1},{1,0},{2,3},{3,2},{4,5},{5,4},{6,7},{7,6},{8,9},{9,8},{10,11... | collective-permute-start | bytes 18874376 | tf_op jit(solution)/shard_map/ppermute | solution.py:323
  5.7 17.5 %collective-permute-start.5 = (bf16[64,4224]{1,0:T(8,128)(2,1)S(1)}, bf16[64,4224]{1,0:T(8,128)(2,1)S(1)}, u32[]{:S(2)}, u32[]{:S(2)}) collective-permute-start(bf16[64,4224]{1,0:T(8,128)(2,1)S(1)} %get-tuple-element.62), channel_id=1, source_target_pairs={{0,2},{1,3},{2,4},{3,5},{4,6},{5,7},{6,0},{7,1},{8,10},{9,11},{10,... | collective-permute-start | bytes 1622024 | tf_op jit(solution)/shard_map/ppermute | solution.py:317
  8.8 9.7 %collective-permute-start = (bf16[336,512]{1,0:T(8,128)(2,1)S(1)}, bf16[336,512]{1,0:T(8,128)(2,1)S(1)}, u32[]{:S(2)}, u32[]{:S(2)}) collective-permute-start(bf16[336,512]{1,0:T(8,128)(2,1)S(1)} %get-tuple-element.58), channel_id=1, source_target_pairs={{0,8},{8,0},{16,24},{24,16},{1,9},{9,1},{17,25},{25,17},{2,10},{10... | collective-permute-start | bytes 1032200 | tf_op jit(solution)/shard_map/ppermute | solution.py:320
  10.3 9.4 %collective-permute-start.1 = (bf16[336,512]{1,0:T(8,128)(2,1)S(1)}, bf16[336,512]{1,0:T(8,128)(2,1)S(1)}, u32[]{:S(2)}, u32[]{:S(2)}) collective-permute-start(bf16[336,512]{1,0:T(8,128)(2,1)S(1)} %get-tuple-element.59), channel_id=1, source_target_pairs={{0,16},{8,24},{16,0},{24,8},{1,17},{9,25},{17,1},{25,9},{2,18},{10... | collective-permute-start | bytes 1032200 | tf_op jit(solution)/shard_map/ppermute | solution.py:320
  24.9 18.9 %collective-permute-start.6 = (bf16[1,768,4096]{2,1,0:T(8,128)(2,1)S(1)}, bf16[1,768,4096]{2,1,0:T(8,128)(2,1)S(1)}, u32[]{:S(2)}, u32[]{:S(2)}) collective-permute-start(bf16[1,768,4096]{2,1,0:T(8,128)(2,1)S(1)} %bitcast.5), channel_id=1, source_target_pairs={{0,1},{1,0},{2,3},{3,2},{4,5},{5,4},{6,7},{7,6},{8,9},{9,8},{10,11... | collective-permute-start | bytes 18874376 | tf_op jit(solution)/shard_map/ppermute | solution.py:323
  25.0 16.5 %collective-permute-start.7 = (bf16[64,4224]{1,0:T(8,128)(2,1)S(1)}, bf16[64,4224]{1,0:T(8,128)(2,1)S(1)}, u32[]{:S(2)}, u32[]{:S(2)}) collective-permute-start(bf16[64,4224]{1,0:T(8,128)(2,1)S(1)} %collective-permute-done.5.wide_ref), channel_id=1, source_target_pairs={{0,2},{1,3},{2,4},{3,5},{4,6},{5,7},{6,0},{7,1},{8,10},{9,11},{10,... | collective-permute-start | bytes 1622024 | tf_op jit(solution)/shard_map/ppermute | solution.py:317
  25.1 16.4 %collective-permute-start.2 = (bf16[336,512]{1,0:T(8,128)(2,1)S(1)}, bf16[336,512]{1,0:T(8,128)(2,1)S(1)}, u32[]{:S(2)}, u32[]{:S(2)}) collective-permute-start(bf16[336,512]{1,0:T(8,128)(2,1)S(1)} %get-tuple-element.61), channel_id=1, source_target_pairs={{0,24},{8,16},{16,8},{24,0},{1,25},{9,17},{17,9},{25,1},{2,26},{10... | collective-permute-start | bytes 1032200 | tf_op jit(solution)/shard_map/ppermute | solution.py:320
  27.6 16.2 %collective-permute-start.8 = (bf16[336,512]{1,0:T(8,128)(2,1)S(1)}, bf16[336,512]{1,0:T(8,128)(2,1)S(1)}, u32[]{:S(2)}, u32[]{:S(2)}) collective-permute-start(bf16[336,512]{1,0:T(8,128)(2,1)S(1)} %get-tuple-element.65), channel_id=1, source_target_pairs={{0,8},{8,0},{16,24},{24,16},{1,9},{9,1},{17,25},{25,17},{2,10},{10... | collective-permute-start | bytes 1032200 | tf_op jit(solution)/shard_map/ppermute | solution.py:320
  28.1 15.7 %collective-permute-start.9 = (bf16[336,512]{1,0:T(8,128)(2,1)S(1)}, bf16[336,512]{1,0:T(8,128)(2,1)S(1)}, u32[]{:S(2)}, u32[]{:S(2)}) collective-permute-start(bf16[336,512]{1,0:T(8,128)(2,1)S(1)} %get-tuple-element.66), channel_id=1, source_target_pairs={{0,16},{8,24},{16,0},{24,8},{1,17},{9,25},{17,1},{25,9},{2,18},{10... | collective-permute-start | bytes 1032200 | tf_op jit(solution)/shard_map/ppermute | solution.py:320
  41.5 25.9 %collective-permute-start.10 = (bf16[64,4224]{1,0:T(8,128)(2,1)S(1)}, bf16[64,4224]{1,0:T(8,128)(2,1)S(1)}, u32[]{:S(2)}, u32[]{:S(2)}) collective-permute-start(bf16[64,4224]{1,0:T(8,128)(2,1)S(1)} %collective-permute-done.7.wide_ref), channel_id=1, source_target_pairs={{0,2},{1,3},{2,4},{3,5},{4,6},{5,7},{6,0},{7,1},{8,10},{9,11},{10,... | collective-permute-start | bytes 1622024 | tf_op jit(solution)/shard_map/ppermute | solution.py:317
  47.5 19.8 %collective-permute-start.12 = (bf16[336,512]{1,0:T(8,128)(2,1)}, bf16[336,512]{1,0:T(8,128)(2,1)S(1)}, u32[]{:S(2)}, u32[]{:S(2)}) collective-permute-start(bf16[336,512]{1,0:T(8,128)(2,1)} %get-tuple-element.72), channel_id=1, source_target_pairs={{0,8},{8,0},{16,24},{24,16},{1,9},{9,1},{17,25},{25,17},{2,10},{10... | collective-permute-start | bytes 1032200 | tf_op jit(solution)/shard_map/ppermute | solution.py:320
  49.0 18.3 %collective-permute-start.11 = (bf16[336,512]{1,0:T(8,128)(2,1)S(1)}, bf16[336,512]{1,0:T(8,128)(2,1)S(1)}, u32[]{:S(2)}, u32[]{:S(2)}) collective-permute-start(bf16[336,512]{1,0:T(8,128)(2,1)S(1)} %get-tuple-element.71), channel_id=1, source_target_pairs={{0,24},{8,16},{16,8},{24,0},{1,25},{9,17},{17,9},{25,1},{2,26},{10... | collective-permute-start | bytes 1032200 | tf_op jit(solution)/shard_map/ppermute | solution.py:320
  50.4 17.0 %collective-permute-start.13 = (bf16[336,512]{1,0:T(8,128)(2,1)}, bf16[336,512]{1,0:T(8,128)(2,1)S(1)}, u32[]{:S(2)}, u32[]{:S(2)}) collective-permute-start(bf16[336,512]{1,0:T(8,128)(2,1)} %get-tuple-element.73), channel_id=1, source_target_pairs={{0,16},{8,24},{16,0},{24,8},{1,17},{9,25},{17,1},{25,9},{2,18},{10... | collective-permute-start | bytes 1032200 | tf_op jit(solution)/shard_map/ppermute | solution.py:320
  71.0 16.8 %collective-permute-start.14 = (bf16[336,512]{1,0:T(8,128)(2,1)S(1)}, bf16[336,512]{1,0:T(8,128)(2,1)S(1)}, u32[]{:S(2)}, u32[]{:S(2)}) collective-permute-start(bf16[336,512]{1,0:T(8,128)(2,1)S(1)} %get-tuple-element.75), channel_id=1, source_target_pairs={{0,8},{8,0},{16,24},{24,16},{1,9},{9,1},{17,25},{25,17},{2,10},{10... | collective-permute-start | bytes 1032200 | tf_op jit(solution)/shard_map/ppermute | solution.py:320
  72.5 17.7 %collective-permute-start.20 = (bf16[336,512]{1,0:T(8,128)(2,1)S(1)}, bf16[336,512]{1,0:T(8,128)(2,1)S(1)}, u32[]{:S(2)}, u32[]{:S(2)}) collective-permute-start(bf16[336,512]{1,0:T(8,128)(2,1)S(1)} %get-tuple-element.91), channel_id=1, source_target_pairs={{0,24},{8,16},{16,8},{24,0},{1,25},{9,17},{17,9},{25,1},{2,26},{10... | collective-permute-start | bytes 1032200 | tf_op jit(solution)/shard_map/ppermute | solution.py:320
  84.2 17.4 %collective-permute-start.17 = (bf16[336,512]{1,0:T(8,128)(2,1)}, bf16[336,512]{1,0:T(8,128)(2,1)S(1)}, u32[]{:S(2)}, u32[]{:S(2)}) collective-permute-start(bf16[336,512]{1,0:T(8,128)(2,1)} %get-tuple-element.87), channel_id=1, source_target_pairs={{0,8},{8,0},{16,24},{24,16},{1,9},{9,1},{17,25},{25,17},{2,10},{10... | collective-permute-start | bytes 1032200 | tf_op jit(solution)/shard_map/ppermute | solution.py:320
  85.7 26.0 %collective-permute-start.18 = (bf16[336,512]{1,0:T(8,128)(2,1)}, bf16[336,512]{1,0:T(8,128)(2,1)S(1)}, u32[]{:S(2)}, u32[]{:S(2)}) collective-permute-start(bf16[336,512]{1,0:T(8,128)(2,1)} %get-tuple-element.88), channel_id=1, source_target_pairs={{0,16},{8,24},{16,0},{24,8},{1,17},{9,25},{17,1},{25,9},{2,18},{10... | collective-permute-start | bytes 1032200 | tf_op jit(solution)/shard_map/ppermute | solution.py:320
  86.4 26.0 %collective-permute-start.19 = (bf16[336,512]{1,0:T(8,128)(2,1)}, bf16[336,512]{1,0:T(8,128)(2,1)S(1)}, u32[]{:S(2)}, u32[]{:S(2)}) collective-permute-start(bf16[336,512]{1,0:T(8,128)(2,1)} %get-tuple-element.89), channel_id=1, source_target_pairs={{0,24},{8,16},{16,8},{24,0},{1,25},{9,17},{17,9},{25,1},{2,26},{10... | collective-permute-start | bytes 1032200 | tf_op jit(solution)/shard_map/ppermute | solution.py:320
  87.8 39.0 %collective-permute-start.15 = (bf16[336,512]{1,0:T(8,128)(2,1)S(1)}, bf16[336,512]{1,0:T(8,128)(2,1)S(1)}, u32[]{:S(2)}, u32[]{:S(2)}) collective-permute-start(bf16[336,512]{1,0:T(8,128)(2,1)S(1)} %get-tuple-element.76), channel_id=1, source_target_pairs={{0,16},{8,24},{16,0},{24,8},{1,17},{9,25},{17,1},{25,9},{2,18},{10... | collective-permute-start | bytes 1032200 | tf_op jit(solution)/shard_map/ppermute | solution.py:320
  90.2 40.1 %collective-permute-start.16 = (bf16[336,512]{1,0:T(8,128)(2,1)S(1)}, bf16[336,512]{1,0:T(8,128)(2,1)S(1)}, u32[]{:S(2)}, u32[]{:S(2)}) collective-permute-start(bf16[336,512]{1,0:T(8,128)(2,1)S(1)} %get-tuple-element.78), channel_id=1, source_target_pairs={{0,24},{8,16},{16,8},{24,0},{1,25},{9,17},{17,9},{25,1},{2,26},{10... | collective-permute-start | bytes 1032200 | tf_op jit(solution)/shard_map/ppermute | solution.py:320
  101.6 40.7 %collective-permute-start.25 = (bf16[336,512]{1,0:T(8,128)(2,1)}, bf16[336,512]{1,0:T(8,128)(2,1)S(1)}, u32[]{:S(2)}, u32[]{:S(2)}) collective-permute-start(bf16[336,512]{1,0:T(8,128)(2,1)} %get-tuple-element.100), channel_id=1, source_target_pairs={{0,8},{8,0},{16,24},{24,16},{1,9},{9,1},{17,25},{25,17},{2,10},{10... | collective-permute-start | bytes 1032200 | tf_op jit(solution)/shard_map/ppermute | solution.py:320
  111.7 31.0 %collective-permute-start.26 = (bf16[336,512]{1,0:T(8,128)(2,1)}, bf16[336,512]{1,0:T(8,128)(2,1)S(1)}, u32[]{:S(2)}, u32[]{:S(2)}) collective-permute-start(bf16[336,512]{1,0:T(8,128)(2,1)} %get-tuple-element.101), channel_id=1, source_target_pairs={{0,16},{8,24},{16,0},{24,8},{1,17},{9,25},{17,1},{25,9},{2,18},{10... | collective-permute-start | bytes 1032200 | tf_op jit(solution)/shard_map/ppermute | solution.py:320
  112.4 32.3 %collective-permute-start.27 = (bf16[336,512]{1,0:T(8,128)(2,1)}, bf16[336,512]{1,0:T(8,128)(2,1)S(1)}, u32[]{:S(2)}, u32[]{:S(2)}) collective-permute-start(bf16[336,512]{1,0:T(8,128)(2,1)} %get-tuple-element.102), channel_id=1, source_target_pairs={{0,24},{8,16},{16,8},{24,0},{1,25},{9,17},{17,9},{25,1},{2,26},{10... | collective-permute-start | bytes 1032200 | tf_op jit(solution)/shard_map/ppermute | solution.py:320
  126.8 35.5 %collective-permute-start.24 = (bf16[64,4096]{1,0:T(8,128)(2,1)S(1)}, bf16[64,4096]{1,0:T(8,128)(2,1)S(1)}, u32[]{:S(2)}, u32[]{:S(2)}) collective-permute-start(bf16[64,4096]{1,0:T(8,128)(2,1)S(1)} %combine.4.refs_10_), channel_id=1, source_target_pairs={{0,6},{1,7},{2,0},{3,1},{4,2},{5,3},{6,4},{7,5},{8,14},{9,15},{10,... | collective-permute-start | bytes 1572872 | tf_op jit(solution)/shard_map/ppermute | solution.py:317
  141.2 7.6 %collective-permute-start.29 = (bf16[336,512]{1,0:T(8,128)(2,1)}, bf16[336,512]{1,0:T(8,128)(2,1)S(1)}, u32[]{:S(2)}, u32[]{:S(2)}) collective-permute-start(bf16[336,512]{1,0:T(8,128)(2,1)} %get-tuple-element.104), channel_id=1, source_target_pairs={{0,8},{8,0},{16,24},{24,16},{1,9},{9,1},{17,25},{25,17},{2,10},{10... | collective-permute-start | bytes 1032200 | tf_op jit(solution)/shard_map/ppermute | solution.py:320
  142.2 10.3 %collective-permute-start.30 = (bf16[336,512]{1,0:T(8,128)(2,1)}, bf16[336,512]{1,0:T(8,128)(2,1)S(1)}, u32[]{:S(2)}, u32[]{:S(2)}) collective-permute-start(bf16[336,512]{1,0:T(8,128)(2,1)} %get-tuple-element.105), channel_id=1, source_target_pairs={{0,16},{8,24},{16,0},{24,8},{1,17},{9,25},{17,1},{25,9},{2,18},{10... | collective-permute-start | bytes 1032200 | tf_op jit(solution)/shard_map/ppermute | solution.py:320
  142.7 13.6 %collective-permute-start.31 = (bf16[336,512]{1,0:T(8,128)(2,1)}, bf16[336,512]{1,0:T(8,128)(2,1)S(1)}, u32[]{:S(2)}, u32[]{:S(2)}) collective-permute-start(bf16[336,512]{1,0:T(8,128)(2,1)} %get-tuple-element.106), channel_id=1, source_target_pairs={{0,24},{8,16},{16,8},{24,0},{1,25},{9,17},{17,9},{25,1},{2,26},{10... | collective-permute-start | bytes 1032200 | tf_op jit(solution)/shard_map/ppermute | solution.py:320
  147.5 26.2 %collective-permute-start.28 = (bf16[64,4096]{1,0:T(8,128)(2,1)S(1)}, bf16[64,4096]{1,0:T(8,128)(2,1)S(1)}, u32[]{:S(2)}, u32[]{:S(2)}) collective-permute-start(bf16[64,4096]{1,0:T(8,128)(2,1)S(1)} %combine.5), channel_id=1, source_target_pairs={{0,4},{1,5},{2,6},{3,7},{4,0},{5,1},{6,2},{7,3},{8,12},{9,13},{10,... | collective-permute-start | bytes 1572872 | tf_op jit(solution)/shard_map/ppermute | solution.py:317
  159.2 14.5 %collective-permute-start.32 = (bf16[64,4096]{1,0:T(8,128)(2,1)S(1)}, bf16[64,4096]{1,0:T(8,128)(2,1)S(1)}, u32[]{:S(2)}, u32[]{:S(2)}) collective-permute-start(bf16[64,4096]{1,0:T(8,128)(2,1)S(1)} %combine.6), channel_id=1, source_target_pairs={{0,2},{1,3},{2,4},{3,5},{4,6},{5,7},{6,0},{7,1},{8,10},{9,11},{10,... | collective-permute-start | bytes 1572872 | tf_op jit(solution)/shard_map/ppermute | solution.py:317
  159.9 10.8 %collective-permute-start.22 = (bf16[336,512]{1,0:T(8,128)(2,1)S(1)}, bf16[336,512]{1,0:T(8,128)(2,1)S(1)}, u32[]{:S(2)}, u32[]{:S(2)}) collective-permute-start(bf16[336,512]{1,0:T(8,128)(2,1)S(1)} %copy-done.27), channel_id=1, source_target_pairs={{0,16},{8,24},{16,0},{24,8},{1,17},{9,25},{17,1},{25,9},{2,18},{10... | collective-permute-start | bytes 1032200 | tf_op jit(solution)/shard_map/ppermute | solution.py:320
  162.2 8.9 %collective-permute-start.23 = (bf16[336,512]{1,0:T(8,128)(2,1)S(1)}, bf16[336,512]{1,0:T(8,128)(2,1)S(1)}, u32[]{:S(2)}, u32[]{:S(2)}) collective-permute-start(bf16[336,512]{1,0:T(8,128)(2,1)S(1)} %copy-done.26), channel_id=1, source_target_pairs={{0,24},{8,16},{16,8},{24,0},{1,25},{9,17},{17,9},{25,1},{2,26},{10... | collective-permute-start | bytes 1032200 | tf_op jit(solution)/shard_map/ppermute | solution.py:320
  (32 other events, 458.0 us)

commit v2 on v1

--- a/solution.py
+++ b/solution.py
@@ -11,8 +11,25 @@
 FOLD = 8
 SUB = 16
 TILE = 256
+SEQUENCE = ["P1", "P2", "E0", "P3", "E2", "E1", "C2", "E3", "C1", "C3"]
+DEPS = {
+    "S2": ["P1"],
+    "P1": ["F0.1", "F0.2", "S0", "S1"],
+    "F0.3": ["P1"],
+    "F1.3": ["P2"],
+    "P2": ["F0.3", "F1.1", "F1.2", "S2"],
+    "P3": ["F1.3", "F2.1", "F2.2", "F2.3"],
+    "R2.1": ["F3.1"],
+    "R2.2": ["F3.2"],
+    "R2.3": ["F3.3"],
+    "R0.1": ["C1"],
+    "R0.2": ["C1"],
+    "R0.3": ["C1"],
+}
+VIA = {}
 F32 = jnp.float32
 BF16 = jnp.bfloat16
+COST = pl.CostEstimate(flops=10**11, transcendentals=0, bytes_accessed=10**8)
 VMEM = pl.BlockSpec(memory_space=pltpu.VMEM)
 SMEM = pl.BlockSpec(memory_space=pltpu.SMEM)
 ANY = pl.BlockSpec(memory_space=pl.ANY)
@@ -28,35 +45,50 @@
     return main, tail, main + (SUB if tail else 0)
 
 
-def unfold(block, cap, rows_ref, base):
+def unfold(blocks, cap, rows_ref):
     main, tail, high = heights(cap)
-    part = block.shape[1]
+    part = blocks[0].shape[1]
     if tail:
         shape = (FOLD * SUB, FOLD * tail)
         r, c = iota(shape, 0), iota(shape, 1)
         spread = ((r % SUB < tail) & (c == r // SUB * tail + r % SUB)).astype(BF16)
-        last = jnp.dot(spread, block[FOLD * main :, :], preferred_element_type=F32).astype(BF16)
-    for g in range(FOLD):
-        cols = slice(g * part, (g + 1) * part)
-        if main:
-            rows_ref[base : base + main, cols] = block[g * main : (g + 1) * main, :]
-        if tail:
-            rows_ref[base + main : base + high, cols] = last[g * SUB : (g + 1) * SUB]
-
-
-def fold(rows_ref, base, cap, block):
+        ends = jnp.concatenate([block[FOLD * main :, :] for block in blocks], axis=1)
+        last = jnp.dot(spread, ends, preferred_element_type=F32).astype(BF16)
+    for m, block in enumerate(blocks):
+        base = m * high
+        for g in range(FOLD):
+            cols = slice(g * part, (g + 1) * part)
+            if main:
+                rows_ref[base : base + main, cols] = block[g * main : (g + 1) * main, :]
+            if tail:
+                rows_ref[base + main : base + high, cols] = last[
+                    g * SUB : (g + 1) * SUB, m * part : (m + 1) * part
+                ]
+
+
+def fold(rows_ref, cap, blocks):
     main, tail, high = heights(cap)
-    part = block.shape[1]
+    part = blocks[0].shape[1]
     columns = [slice(g * part, (g + 1) * part) for g in range(FOLD)]
-    if main:
-        for g, cols in enumerate(columns):
-            block[g * main : (g + 1) * main, :] = rows_ref[base : base + main, cols]
     if tail:
-        last = jnp.concatenate([rows_ref[base + main : base + high, cols] for cols in columns], axis=0)
+        starts = [m * high + main for m in range(len(blocks))]
+        last = jnp.concatenate(
+            [
+                jnp.concatenate([rows_ref[at : at + SUB, cols] for cols in columns], axis=0)
+                for at in starts
+            ],
+            axis=1,
+        )
         shape = (FOLD * tail, FOLD * SUB)
         r, c = iota(shape, 0), iota(shape, 1)
         gather = ((c % SUB < tail) & (r == c // SUB * tail + c % SUB)).astype(BF16)
-        block[FOLD * main :, :] = jnp.dot(gather, last, preferred_element_type=F32).astype(BF16)
+        ends = jnp.dot(gather, last, preferred_element_type=F32).astype(BF16)
+    for m, block in enumerate(blocks):
+        if main:
+            for g, cols in enumerate(columns):
+                block[g * main : (g + 1) * main, :] = rows_ref[m * high : m * high + main, cols]
+        if tail:
+            block[FOLD * main :, :] = ends[:, m * part : (m + 1) * part]
 
 
 def slot_codes(weights):
@@ -85,8 +117,7 @@
         picks.append((iota((high, tokens), 0) == row).astype(BF16))
     pick = jnp.concatenate(picks, axis=0)
     rows_ref[...] = jnp.dot(pick, x_ref[...], preferred_element_type=F32).astype(BF16)
-    for m, out in enumerate(outs):
-        fold(rows_ref, m * high, cap, out)
+    fold(rows_ref, cap, outs)
 
 
 def tie(value, *others):
@@ -99,23 +130,26 @@
 
 def first_kernel(n, cap, ids_ref, x_ref, routes_ref, gate_ref, *refs):
     w_ref, wide_ref, outs, rows_ref = refs[0], refs[1], refs[2 : 2 + n], refs[2 + n]
+    tokens, width = x_ref.shape
+    count = w_ref.shape[1]
     quant = gate_ref[...].astype(F32)
-    chosen = quant / jnp.sum(quant, axis=1, keepdims=True)
+    chosen = quant / jnp.sum(quant, axis=0, keepdims=True)
     routes = routes_ref[...]
-    experts = iota(w_ref.shape, 1)
-    weights = jnp.zeros(w_ref.shape, F32)
+    experts = iota((count, tokens), 0)
+    turned = jnp.zeros((count, tokens), F32)
     for k in range(TOP):
-        weights += jnp.where(experts == routes[:, k : k + 1], chosen[:, k : k + 1], 0.0)
+        turned += jnp.where(experts == routes[k : k + 1, :], chosen[k : k + 1, :], 0.0)
+    unit = (iota((tokens, tokens), 0) == iota((tokens, tokens), 1)).astype(BF16)
+    terms, rest = [], turned
+    for _ in range(3):
+        term = rest.astype(BF16)
+        rest = rest - term.astype(F32)
+        terms.append(lax.dot_general(unit, term, (((1,), (1,)), ((), ())), preferred_element_type=F32))
+    weights = terms[0] + terms[1] + terms[2]
     w_ref[...] = weights
-    width, count = x_ref.shape[1], w_ref.shape[1]
     wide_ref[:, :width] = x_ref[...]
-    terms, rest = [], weights
-    for _ in range(3):
-        terms.append(rest.astype(BF16))
-        rest = rest - terms[-1].astype(F32)
-    fill = wide_ref.shape[1] - width - 3 * count
-    terms.append(jnp.zeros((w_ref.shape[0], fill), BF16))
-    wide_ref[:, width:] = jnp.concatenate(terms, axis=1)
+    terms.append(jnp.zeros((tokens, wide_ref.shape[1] - width - 3 * count), F32))
+    wide_ref[:, width:] = jnp.concatenate(terms, axis=1).astype(BF16)
     pack_body(cap, ids_ref, x_ref, weights, outs, rows_ref)
 
 
@@ -133,9 +167,10 @@
         in_specs=[SMEM, VMEM, VMEM, VMEM],
         out_specs=(VMEM,) * (2 + n),
         scratch_shapes=[pltpu.VMEM((n * heights(cap)[2], width), BF16)],
+        cost_estimate=COST,
         compiler_params=pltpu.CompilerParams(vmem_limit_bytes=12 << 20),
         name="first",
-    )(ids, x, routes, gate_fixed)
+    )(ids, x, routes.T, gate_fixed.T)
 
 
 def pack_kernel(n, cap, ids_ref, wide_ref, *refs):
@@ -160,16 +195,15 @@
         in_specs=[SMEM, VMEM] + [ANY] * len(after),
         out_specs=(VMEM,) * (1 + n),
         scratch_shapes=[pltpu.VMEM((n * heights(cap)[2], width), BF16)],
+        cost_estimate=COST,
         compiler_params=pltpu.CompilerParams(vmem_limit_bytes=12 << 20),
         name="pack",
     )(ids, wide, *after)
 
 
-def expert_body(n, cap, blocks, weights, outs, x_ref, h_ref, y_ref, ready):
-    high = heights(cap)[2]
+def expert_body(cap, blocks, weights, outs, x_ref, h_ref, y_ref, ready):
     half, width = weights[2].shape[1:]
-    for m in range(n):
-        unfold(blocks[m], cap, x_ref, m * high)
+    unfold(blocks, cap, x_ref)
     x = x_ref[...]
     steps = expert_steps(half, width)
     for i, (s, j) in enumerate(steps):
@@ -190,8 +224,7 @@
                 for t in range(2)
             )
             y_ref[:, j : j + 2 * TILE] = total.astype(BF16)
-    for m in range(n):
-        fold(y_ref, m * high, cap, outs[m])
+    fold(y_ref, cap, outs)
 
 
 def expert_steps(half, width):
@@ -202,7 +235,7 @@
 def expert_kernel(n, cap, *refs):
     blocks, weights = refs[:n], refs[n : n + 6]
     outs, scratch = refs[-3 - n : -3], refs[-3:]
-    expert_body(n, cap, blocks, weights, outs, *scratch, lambda i: None)
+    expert_body(cap, blocks, weights, outs, *scratch, lambda i: None)
 
 
 def expert_first_kernel(n, cap, *refs):
@@ -236,7 +269,7 @@
     for i in range(depth):
         for copy in copies(i):
             copy.start()
-    expert_body(n, cap, blocks, weights, outs, *scratch, ready)
+    expert_body(cap, blocks, weights, outs, *scratch, ready)
 
 
 def expert(blocks, weights, cap, after=(), first_call=False):
@@ -252,7 +285,7 @@
     if first_call:
         kernel, space, name = expert_first_kernel, ANY, "expert_first"
         out_shape += tuple(pltpu.VMEM(w.shape, w.dtype) for w in weights)
-        scratch.append(pltpu.SemaphoreType.DMA((3, 2)))
+        scratch.append(pltpu.SemaphoreType.DMA((5, 2)))
     else:
         kernel, space, name = expert_kernel, VMEM, "expert"
         weights = [pltpu.with_memory_space_constraint(w, pltpu.VMEM) for w in weights]
@@ -262,6 +295,7 @@
         in_specs=[VMEM] * n + [space] * 6 + [ANY] * len(after),
         out_specs=(VMEM,) * len(out_shape),
         scratch_shapes=scratch,
+        cost_estimate=COST,
         compiler_params=pltpu.CompilerParams(vmem_limit_bytes=18 << 20),
         name=name,
     )(*blocks, *weights, *after)
@@ -276,8 +310,8 @@
     weights = w_ref[...]
     codes = slot_codes(weights)
     total = None
+    unfold(blocks, cap, rows_ref)
     for m in range(n):
-        unfold(blocks[m], cap, rows_ref, m * high)
         code = column(codes, ids_ref[m]).astype(jnp.int32)
         pick = (code == iota((tokens, high), 1)).astype(BF16)
         rows = jnp.dot(pick, rows_ref[m * high : (m + 1) * high, :], preferred_element_type=F32)
@@ -297,9 +331,18 @@
         in_specs=[SMEM] + [VMEM] * (1 + n + len(others)) + [ANY] * len(after),
         out_specs=VMEM,
         scratch_shapes=[pltpu.VMEM((n * heights(cap)[2], width), BF16)],
+        cost_estimate=COST,
         compiler_params=pltpu.CompilerParams(vmem_limit_bytes=12 << 20),
         name="combine",
     )(ids, weights, *blocks, *others, *after)
+
+
+def plan(line, n_data):
+    if line == 4 and n_data == 4:
+        return SEQUENCE, DEPS, VIA
+    far = sorted(range(1, line), key=lambda k: (-min(k, line - k), k))
+    steps = [f"P{k}" for k in range(1, line)] + [f"E{k}" for k in far + [0]]
+    return steps + [f"C{k}" for k in far], {}, {}
 
 
 def on_device(tokens, routes, gate_fixed, w_gate, w_up, w_down):
@@ -311,6 +354,8 @@
     dp = lax.axis_index("dp")
     z = lax.axis_index("expert") // 2
     ids = jnp.stack([(dp ^ m) * line + z for m in range(n_data)]).astype(jnp.int32)
+    sequence, deps, via = plan(line, n_data)
+    made = {}
 
     def along(block, step):
         pairs = [(i, (i + 2 * step) % n_owner) for i in range(n_owner)]
@@ -322,53 +367,57 @@
     def swap(block):
         return lax.ppermute(block, "expert", [(i, i ^ 1) for i in range(n_owner)])
 
-    last = n_data - 1
-
-    def exchange(lists, after=None):
-        got = [lists[0]] + [across(lists[m], m) for m in range(1, last)]
-        if last:
-            got.append(across(tie(lists[last], *got[1:2]), last))
-        return got
-
-    weights, wide, *lists = first(tokens, routes, gate_fixed, ids, cap, expert_count)
-    other = [swap(w_gate), swap(w_up)]
-    ws, sent = [weights], [exchange(lists)]
-    after = (*sent[0][1:last], *other)
-    for k in range(1, line):
-        wide = along(wide, 1)
-        weights, *lists = pack(wide, ids, cap, expert_count, after=after)
-        ws.append(weights)
-        sent.append(exchange(lists))
-        after = (*sent[k - 1][last:], *sent[k][1:last])
-        if k == 1:
-            other.append(swap(tie(w_down, lists[0])))
-            after += (other[2],)
-        if k == 2:
-            held = [w_gate, w_up, w_down, *other]
-            outs, held = expert(sent[0], held, cap, after=(lists[0],), first_call=True)
-            result = {0: outs}
-            after += (outs[0],)
-
-    after = lists[:1]
-    order = list(range(1, line))
-    back = {}
-
-    def send_back(k, after):
-        part = combine(result[k], ws[k], ids, cap, after=after)
-        back[k] = along(part, -k)
-        return [part]
-
-    for i, k in enumerate(order):
-        if i >= 2:
-            after = send_back(order[i - 2], after)
-        outs, _ = expert(sent[k], held, cap, after=after)
-        after = outs[:1]
-        result[k] = [outs[0]] + [across(outs[m], m) for m in range(1, n_data)]
-    result[0] = [result[0][0]] + [across(tie(result[0][m], after[0]), m) for m in range(1, n_data)]
-    for k in order:
-        if k not in back:
-            send_back(k, after)
-    return combine(result[0], ws[0], ids, cap, others=list(back.values()))
+    def marks(name):
+        step = get(name)
+        return step if isinstance(step, jax.Array) else step[-1]
+
+    def after(name):
+        at = sequence.index(name) if name in sequence else 0
+        return [marks(d) for d in [*sequence[:at][-1:], *deps.get(name, ())]]
+
+    def held(value, name):
+        others = [marks(d) for d in deps.get(name, ())]
+        return tie(value, *others) if others else value
+
+    def lists(kind, k):
+        source = get(("P" if kind == "F" else "E") + str(k))
+        return [source[0]] + [get(f"{kind}{k}.{m}") for m in range(1, n_data)]
+
+    def get(name):
+        if name not in made:
+            made[name] = make(name, name[0], *map(int, name[1:].split(".")))
+        return made[name]
+
+    def make(name, kind, k, m=0):
+        if kind == "S":
+            return swap(held((w_gate, w_up, w_down)[k], name))
+        if kind == "X":
+            return along(held(get("P0")[-2] if k == 1 else get(f"X{k - 1}"), name), 1)
+        if kind == "P" and k == 0:
+            weights, wide, *outs = first(tokens, routes, gate_fixed, ids, cap, expert_count)
+            return [*outs, weights, wide, outs[0]]
+        if kind == "P":
+            weights, *outs = pack(get(f"X{k}"), ids, cap, expert_count, after=after(name))
+            return [*outs, weights, outs[0]]
+        if kind in "FR":
+            return across(held(get(("P" if kind == "F" else "E") + str(k))[m], name), m)
+        if kind == "E":
+            opening = next(s for s in sequence if s[0] == "E")
+            if name == opening:
+                weights = [w_gate, w_up, w_down] + [get(f"S{i}") for i in range(3)]
+            else:
+                weights = get(opening)[n_data:-1]
+            outs, kept = expert(lists("F", k), weights, cap, after=after(name), first_call=name == opening)
+            return [*outs, *kept, outs[0]]
+        if kind == "C":
+            others = [get(f"H{far}") for far, near in via.items() if near == k]
+            return combine(lists("R", k), get(f"P{k}")[n_data], ids, cap, others=others, after=after(name))
+        return along(held(get(f"C{k}"), name), via.get(k, 0) - k)
+
+    for name in sequence:
+        get(name)
+    ends = [get(f"H{k}") for k in range(1, line) if k not in via]
+    return combine(lists("R", 0), get("P0")[n_data], ids, cap, others=ends)
 
 
 def solution(mesh):

time: 177 us -> 163 us (0.921)
  waiting for transfers between devices: 67.3 us -> 47.8 us
  starting transfers between devices: 35.8 us -> 40.3 us
    ppermute x24, waiting for transfers between devices: 48.3 us -> 31.3 us  [across(): return lax.ppermute(block, 'dp', [(i, i ^ m) for i in range(n_data)])]
    ppermute x6, waiting for transfers between devices: 19 us -> 16.5 us  [along(): return lax.ppermute(block, 'expert', pairs)]
    ppermute x6, starting transfers between devices: 6.75 us -> 9.09 us  [along(): return lax.ppermute(block, 'expert', pairs)]
    ppermute x24, starting transfers between devices: 28.4 us -> 30.6 us  [across(): return lax.ppermute(block, 'dp', [(i, i ^ m) for i in range(n_data)])]
  transfers between devices with their start and end apart: 33 -> 33, of which waited for: 15 -> 11; matrix products, arithmetic and copies ran while one was open for 1% -> 0% of each run, Pallas kernels for 32% -> 35%
where the time goes in v2:
time: 163 us
  Pallas kernels  64.2 us (39%)
  waiting for transfers between devices  47.8 us (29%)
  starting transfers between devices  40.3 us (25%)
  local copies, waits for them, and re-layouts  10.1 us (6%)
    pallas_call x4, Pallas kernels, expert(): pl.pallas_call(functools.partial(kernel, n, cap), out_shape=out_shape, in...  47.3 us
    ppermute x24, waiting for transfers between devices, across(): return lax.ppermute(block, 'dp', [(i, i ^ m) for i in range(n_data)])  31.3 us
    ppermute x24, starting transfers between devices, across(): return lax.ppermute(block, 'dp', [(i, i ^ m) for i in range(n_data)])  30.6 us
    ppermute x6, waiting for transfers between devices, along(): return lax.ppermute(block, 'expert', pairs)  16.5 us
    unnamed x64, local copies, waits for them, and re-layouts  10.1 us
    ppermute x6, starting transfers between devices, along(): return lax.ppermute(block, 'expert', pairs)  9.09 us
    pallas_call x4, Pallas kernels, combine(): pl.pallas_call(functools.partial(combine_kernel, n, len(others), cap), ou...  8.94 us
    pallas_call x3, Pallas kernels, pack(): pl.pallas_call(functools.partial(pack_kernel, n, cap), out_shape=(jax.Sha...  6.32 us
  transfers between devices with their start and end apart: 33, of which 11 were waited for; matrix products, arithmetic and copies ran while one was open for 0% of the time, Pallas kernels for 35%

profile of v2, /device:TPU:0, one launch (start us, length us, event | category | flops | bytes accessed | tf_op | source)
XLA Modules:
  0.0 162.8 jit_solution(11302530480250985741)
XLA Ops:
  3.0 1.6 %first.1 = (f32[64,16]{1,0:T(8,128)S(1)}, bf16[64,4224]{1,0:T(8,128)(2,1)S(1)}, bf16[336,512]{1,0:T(8,128)(2,1)S(1)}, bf16[336,512]{1,0:T(8,128)(2,1)S(1)}, bf16...) custom-call(s32[4]{0:T(128)S(1)} %pad_add_fusion.ids_ref, bf16[64,4096]{1,0:T(8,128)(2,1)S(1)} %copy-done.1, ...), custom_call_target="tpu_custom_call" | custom-call | flops 99999997952 | bytes 100000000 | tf_op jit(solution)/shard_map/first/pallas_call | solution.py:160
  5.4 3.0 %collective-permute-start.2 = (bf16[64,4224]{1,0:T(8,128)(2,1)S(1)}, bf16[64,4224]{1,0:T(8,128)(2,1)S(1)}, u32[]{:S(2)}, u32[]{:S(2)}) collective-permute-start(bf16[64,4224]{1,0:T(8,128)(2,1)S(1)} %get-tuple-element.62), channel_id=1, source_target_pairs={{0,2},{1,3},{2,4},{3,5},{4,6},{5,7},{6,0},{7,1},{8,10},{9,11},{10,... | collective-permute-start | bytes 1622024 | tf_op jit(solution)/shard_map/ppermute | solution.py:362
  9.9 1.5 collective-permute-start.1
  11.4 6.7 %collective-permute-done.refs_0_.refs_1_ = bf16[336,512]{1,0:T(8,128)(2,1)S(1)} collective-permute-done((bf16[336,512]{1,0:T(8,128)(2,1)S(1)}, bf16[336,512]{1,0:T(8,128)(2,1)S(1)}, u32[]{:S(2)}, u32[]{:S(2)}) %collective-permute-start) | collective-permute-done | bytes 344096 | tf_op jit(solution)/shard_map/ppermute | solution.py:365
  19.3 3.6 %collective-permute-done.2.wide_ref = bf16[64,4224]{1,0:T(8,128)(2,1)S(1)} collective-permute-done((bf16[64,4224]{1,0:T(8,128)(2,1)S(1)}, bf16[64,4224]{1,0:T(8,128)(2,1)S(1)}, u32[]{:S(2)}, u32[]{:S(2)}) %collective-permute-start.2) | collective-permute-done | bytes 540704 | tf_op jit(solution)/shard_map/ppermute | solution.py:362
  22.9 1.6 pack.3
  24.7 2.5 %collective-permute-start.5 = (bf16[336,512]{1,0:T(8,128)(2,1)S(1)}, bf16[336,512]{1,0:T(8,128)(2,1)S(1)}, u32[]{:S(2)}, u32[]{:S(2)}) collective-permute-start(bf16[336,512]{1,0:T(8,128)(2,1)S(1)} %get-tuple-element.64), channel_id=1, source_target_pairs={{0,24},{8,16},{16,8},{24,0},{1,25},{9,17},{17,9},{25,1},{2,26},{10... | collective-permute-start | bytes 1032200 | tf_op jit(solution)/shard_map/ppermute | solution.py:365
  28.3 12.9 %collective-permute-done.7.wide_ref = bf16[64,4224]{1,0:T(8,128)(2,1)} collective-permute-done((bf16[64,4224]{1,0:T(8,128)(2,1)S(1)}, bf16[64,4224]{1,0:T(8,128)(2,1)}, u32[]{:S(2)}, u32[]{:S(2)}) %collective-permute-start.7) | collective-permute-done | bytes 540704 | tf_op jit(solution)/shard_map/ppermute | solution.py:362
  41.2 2.2 %collective-permute-done.8.refs_2_.refs_1_ = bf16[336,512]{1,0:T(8,128)(2,1)S(1)} collective-permute-done((bf16[336,512]{1,0:T(8,128)(2,1)S(1)}, bf16[336,512]{1,0:T(8,128)(2,1)S(1)}, u32[]{:S(2)}, u32[]{:S(2)}) %collective-permute-start.8) | collective-permute-done | bytes 344096 | tf_op jit(solution)/shard_map/ppermute | solution.py:365
  43.5 2.6 %pack.4 = (f32[64,16]{1,0:T(8,128)S(1)}, bf16[336,512]{1,0:T(8,128)(2,1)S(1)}, bf16[336,512]{1,0:T(8,128)(2,1)S(1)}, bf16[336,512]{1,0:T(8,128)(2,1)S(1)}, bf16[336,512]{1,0:T(8,128)(2,1)S(1)}) custom-call(s32[4]{0:T(128)S(1)} %pad_add_fusion.ids_ref, bf16[64,4224]{1,0:T(8,128)(2,1)} %collective-permute-done.7.wide_ref, ...), custom_call_target="tpu_custom_call" | custom-call | flops 99999997952 | bytes 100000000 | tf_op jit(solution)/shard_map/pack/pallas_call | solution.py:192
  47.0 2.2 %collective-permute-start.10 = (bf16[336,512]{1,0:T(8,128)(2,1)S(1)}, bf16[336,512]{1,0:T(8,128)(2,1)S(1)}, u32[]{:S(2)}, u32[]{:S(2)}) collective-permute-start(bf16[336,512]{1,0:T(8,128)(2,1)S(1)} %get-tuple-element.73), channel_id=1, source_target_pairs={{0,24},{8,16},{16,8},{24,0},{1,25},{9,17},{17,9},{25,1},{2,26},{10... | collective-permute-start | bytes 1032200 | tf_op jit(solution)/shard_map/ppermute | solution.py:365
  50.5 2.2 %collective-permute-start.13 = (bf16[336,512]{1,0:T(8,128)(2,1)S(1)}, bf16[336,512]{1,0:T(8,128)(2,1)S(1)}, u32[]{:S(2)}, u32[]{:S(2)}) collective-permute-start(bf16[336,512]{1,0:T(8,128)(2,1)S(1)} %get-tuple-element.82), channel_id=1, source_target_pairs={{0,24},{8,16},{16,8},{24,0},{1,25},{9,17},{17,9},{25,1},{2,26},{10... | collective-permute-start | bytes 1032200 | tf_op jit(solution)/shard_map/ppermute | solution.py:365
  52.7 16.2 %expert_first.1 = (bf16[336,512]{1,0:T(8,128)(2,1)}, bf16[336,512]{1,0:T(8,128)(2,1)}, bf16[336,512]{1,0:T(8,128)(2,1)}, bf16[336,512]{1,0:T(8,128)(2,1)}, bf16[...) custom-call(bf16[336,512]{1,0:T(8,128)(2,1)} %copy-done.19, ...), custom_call_target="tpu_custom_call" | custom-call | flops 99999997952 | bytes 100000000 | tf_op jit(solution)/shard_map/expert_first/pallas_call | solution.py:292
  69.0 3.4 %collective-permute-done.13.refs_4_.refs_3_ = bf16[336,512]{1,0:T(8,128)(2,1)S(1)} collective-permute-done((bf16[336,512]{1,0:T(8,128)(2,1)S(1)}, bf16[336,512]{1,0:T(8,128)(2,1)S(1)}, u32[]{:S(2)}, u32[]{:S(2)}) %collective-permute-start.13) | collective-permute-done | bytes 344096 | tf_op jit(solution)/shard_map/ppermute | solution.py:365
  73.6 2.1 %pack.5 = (f32[64,16]{1,0:T(8,128)S(1)}, bf16[336,512]{1,0:T(8,128)(2,1)S(1)}, bf16[336,512]{1,0:T(8,128)(2,1)S(1)}, bf16[336,512]{1,0:T(8,128)(2,1)S(1)}, bf16[336,512]{1,0:T(8,128)(2,1)S(1)}) custom-call(s32[4]{0:T(128)S(1)} %pad_add_fusion.ids_ref, bf16[64,4224]{1,0:T(8,128)(2,1)} %collective-permute-done.14.wide_ref, bf16[336,512]{1,0:T(8,128)(2,1)S(1)} %copy-done.16, ...), custom_call_target="tpu_custom_call" | custom-call | flops 99999997952 | bytes 100000000 | tf_op jit(solution)/shard_map/pack/pallas_call | solution.py:192
  78.0 1.5 collective-permute-start.19
  80.0 10.4 %expert.3 = (bf16[336,512]{1,0:T(8,128)(2,1)}, bf16[336,512]{1,0:T(8,128)(2,1)}, bf16[336,512]{1,0:T(8,128)(2,1)}, bf16[336,512]{1,0:T(8,128)(2,1)}) custom-call(bf16[336,512]{1,0:T(8,128)(2,1)} %copy-done.22, bf16[336,512]{1,0:T(8,128)(2,1)} %copy-done.7, bf16[336,512]{1,0:T(8,128)(2,1)} %copy-done.9, bf16[336,512]{1,0:T(8,128)(2,1)} %copy-done.10, ...), custom_call_target="tpu_custom_call" | custom-call | flops 99999997952 | bytes 100000000 | tf_op jit(solution)/shard_map/expert/pallas_call | solution.py:292
  94.0 2.5 %collective-permute-start.22 = (bf16[336,512]{1,0:T(8,128)(2,1)}, bf16[336,512]{1,0:T(8,128)(2,1)S(1)}, u32[]{:S(2)}, u32[]{:S(2)}) collective-permute-start(bf16[336,512]{1,0:T(8,128)(2,1)} %get-tuple-element.96), channel_id=1, source_target_pairs={{0,16},{8,24},{16,0},{24,8},{1,17},{9,25},{17,1},{25,9},{2,18},{10... | collective-permute-start | bytes 1032200 | tf_op jit(solution)/shard_map/ppermute | solution.py:365
  97.2 10.2 %expert.4 = (bf16[336,512]{1,0:T(8,128)(2,1)}, bf16[336,512]{1,0:T(8,128)(2,1)}, bf16[336,512]{1,0:T(8,128)(2,1)}, bf16[336,512]{1,0:T(8,128)(2,1)}) custom-call(bf16[336,512]{1,0:T(8,128)(2,1)} %copy-done.18, bf16[336,512]{1,0:T(8,128)(2,1)} %copy-done.2, bf16[336,512]{1,0:T(8,128)(2,1)} %copy-done.3, bf16[336,512]{1,0:T(8,128)(2,1)} %copy-done.4, ...), custom_call_target="tpu_custom_call" | custom-call | flops 99999997952 | bytes 100000000 | tf_op jit(solution)/shard_map/expert/pallas_call | solution.py:292
  108.9 2.0 %collective-permute-start.16 = (bf16[336,512]{1,0:T(8,128)(2,1)}, bf16[336,512]{1,0:T(8,128)(2,1)}, u32[]{:S(2)}, u32[]{:S(2)}) collective-permute-start(bf16[336,512]{1,0:T(8,128)(2,1)} %get-tuple-element.87), channel_id=1, source_target_pairs={{0,16},{8,24},{16,0},{24,8},{1,17},{9,25},{17,1},{25,9},{2,18},{10... | collective-permute-start | bytes 1032200 | tf_op jit(solution)/shard_map/ppermute | solution.py:365
  111.9 2.3 %combine.4.refs_10_ = bf16[64,4096]{1,0:T(8,128)(2,1)} custom-call(s32[4]{0:T(128)S(1)} %pad_add_fusion.ids_ref, f32[64,16]{1,0:T(8,128)S(1)} %get-tuple-element.92.w_ref, bf16[336,512]{1,0:T(8,128)(2,1)S(1)} %copy-done.23, bf16[336,512]{1,0:T(8,128)(2,1)S(1)} %collective-permute-done.21.refs_1_, bf16[336,512]{1,0:T(8,128)(2,1)S(1)} %collective-permute-done.22.refs_2_, ...), custom_call_target="tpu_custom_call" | custom-call | flops 99999997952 | bytes 100000000 | tf_op jit(solution)/shard_map/combine/pallas_call | solution.py:328
  114.2 2.2 %collective-permute-start.28 = (bf16[64,4096]{1,0:T(8,128)(2,1)}, bf16[64,4096]{1,0:T(8,128)(2,1)}, u32[]{:S(2)}, u32[]{:S(2)}) collective-permute-start(bf16[64,4096]{1,0:T(8,128)(2,1)} %combine.4.refs_10_), channel_id=1, source_target_pairs={{0,4},{1,5},{2,6},{3,7},{4,0},{5,1},{6,2},{7,3},{8,12},{9,13},{10,... | collective-permute-start | bytes 1572872 | tf_op jit(solution)/shard_map/ppermute | solution.py:362
  116.4 10.4 %expert.5 = (bf16[336,512]{1,0:T(8,128)(2,1)}, bf16[336,512]{1,0:T(8,128)(2,1)}, bf16[336,512]{1,0:T(8,128)(2,1)}, bf16[336,512]{1,0:T(8,128)(2,1)}) custom-call(bf16[336,512]{1,0:T(8,128)(2,1)} %copy-done.13, bf16[336,512]{1,0:T(8,128)(2,1)} %copy-done.27, bf16[336,512]{1,0:T(8,128)(2,1)} %copy-done.28, bf16[336,512]{1,0:T(8,128)(2,1)} %copy-done.29, ...), custom_call_target="tpu_custom_call" | custom-call | flops 99999997952 | bytes 100000000 | tf_op jit(solution)/shard_map/expert/pallas_call | solution.py:292
  128.3 2.0 %collective-permute-start.30 = (bf16[336,512]{1,0:T(8,128)(2,1)}, bf16[336,512]{1,0:T(8,128)(2,1)S(1)}, u32[]{:S(2)}, u32[]{:S(2)}) collective-permute-start(bf16[336,512]{1,0:T(8,128)(2,1)} %get-tuple-element.107), channel_id=1, source_target_pairs={{0,16},{8,24},{16,0},{24,8},{1,17},{9,25},{17,1},{25,9},{2,18},{10... | collective-permute-start | bytes 1032200 | tf_op jit(solution)/shard_map/ppermute | solution.py:365
  131.3 2.2 %combine.5.refs_4_ = bf16[64,4096]{1,0:T(8,128)(2,1)S(1)} custom-call(s32[4]{0:T(128)S(1)} %pad_add_fusion.ids_ref, f32[64,16]{1,0:T(8,128)S(1)} %get-tuple-element.71.w_ref, bf16[336,512]{1,0:T(8,128)(2,1)S(1)} %copy-done.21, bf16[336,512]{1,0:T(8,128)(2,1)} %collective-permute-done.15.refs_1_, bf16[336,512]{1,0:T(8,128)(2,1)} %collective-permute-done.16.refs_2_, ...), custom_call_target="tpu_custom_call" | custom-call | flops 99999997952 | bytes 100000000 | tf_op jit(solution)/shard_map/combine/pallas_call | solution.py:328
  133.5 1.6 collective-permute-start.27
  135.1 2.9 %collective-permute-done.29.refs_1_ = bf16[336,512]{1,0:T(8,128)(2,1)S(1)} collective-permute-done((bf16[336,512]{1,0:T(8,128)(2,1)}, bf16[336,512]{1,0:T(8,128)(2,1)S(1)}, u32[]{:S(2)}, u32[]{:S(2)}) %collective-permute-start.29) | collective-permute-done | bytes 344096 | tf_op jit(solution)/shard_map/ppermute | solution.py:365
  139.5 5.5 %collective-permute-done.31.refs_3_ = bf16[336,512]{1,0:T(8,128)(2,1)S(1)} collective-permute-done((bf16[336,512]{1,0:T(8,128)(2,1)}, bf16[336,512]{1,0:T(8,128)(2,1)S(1)}, u32[]{:S(2)}, u32[]{:S(2)}) %collective-permute-start.31) | collective-permute-done | bytes 344096 | tf_op jit(solution)/shard_map/ppermute | solution.py:365
  146.6 2.1 %collective-permute-start.32 = (bf16[64,4096]{1,0:T(8,128)(2,1)S(1)}, bf16[64,4096]{1,0:T(8,128)(2,1)S(1)}, u32[]{:S(2)}, u32[]{:S(2)}) collective-permute-start(bf16[64,4096]{1,0:T(8,128)(2,1)S(1)} %combine.6), channel_id=1, source_target_pairs={{0,2},{1,3},{2,4},{3,5},{4,6},{5,7},{6,0},{7,1},{8,10},{9,11},{10,... | collective-permute-start | bytes 1572872 | tf_op jit(solution)/shard_map/ppermute | solution.py:362
  149.6 2.0 %collective-permute-start.26 = (bf16[336,512]{1,0:T(8,128)(2,1)S(1)}, bf16[336,512]{1,0:T(8,128)(2,1)S(1)}, u32[]{:S(2)}, u32[]{:S(2)}) collective-permute-start(bf16[336,512]{1,0:T(8,128)(2,1)S(1)} %copy-done.24), channel_id=1, source_target_pairs={{0,24},{8,16},{16,8},{24,0},{1,25},{9,17},{17,9},{25,1},{2,26},{10... | collective-permute-start | bytes 1032200 | tf_op jit(solution)/shard_map/ppermute | solution.py:365
  151.6 8.1 %collective-permute-done.25.refs_2_ = bf16[336,512]{1,0:T(8,128)(2,1)S(1)} collective-permute-done((bf16[336,512]{1,0:T(8,128)(2,1)S(1)}, bf16[336,512]{1,0:T(8,128)(2,1)S(1)}, u32[]{:S(2)}, u32[]{:S(2)}) %collective-permute-start.25) | collective-permute-done | bytes 344096 | tf_op jit(solution)/shard_map/ppermute | solution.py:365
  159.8 3.0 %combine.7 = bf16[64,4096]{1,0:T(8,128)(2,1)} custom-call(s32[4]{0:T(128)S(1)} %pad_add_fusion.ids_ref, f32[64,16]{1,0:T(8,128)S(1)} %get-tuple-element.57.w_ref, bf16[336,512]{1,0:T(8,128)(2,1)S(1)} %copy-done.17, bf16[336,512]{1,0:T(8,128)(2,1)S(1)} %collective-permute-done.24.refs_1_, bf16[336,512]{1,0:T(8,128)(2,1)S(1)} %collective-permute-done.25.refs_2_, ...), custom_call_target="tpu_custom_call" | custom-call | flops 99999997952 | bytes 100000000 | tf_op jit(solution)/shard_map/combine/pallas_call | solution.py:328
  (112 shorter events, 26.7 us)
Async XLA Ops:
  0.0 22.9 %collective-permute-start.3 = (bf16[1,4096,768]{2,1,0:T(8,128)(2,1)}, bf16[1,4096,768]{2,1,0:T(8,128)(2,1)}, u32[]{:S(2)}, u32[]{:S(2)}) collective-permute-start(bf16[1,4096,768]{2,1,0:T(8,128)(2,1)} %refs_4_.1), channel_id=1, source_target_pairs={{0,1},{1,0},{2,3},{3,2},{4,5},{5,4},{6,7},{7,6},{8,9},{9,8},{10,11... | collective-permute-start | bytes 18874376 | tf_op jit(solution)/shard_map/ppermute | solution.py:368
  0.5 22.4 %collective-permute-start.4 = (bf16[1,4096,768]{2,1,0:T(8,128)(2,1)}, bf16[1,4096,768]{2,1,0:T(8,128)(2,1)}, u32[]{:S(2)}, u32[]{:S(2)}) collective-permute-start(bf16[1,4096,768]{2,1,0:T(8,128)(2,1)} %refs_5_.1), channel_id=1, source_target_pairs={{0,1},{1,0},{2,3},{3,2},{4,5},{5,4},{6,7},{7,6},{8,9},{9,8},{10,11... | collective-permute-start | bytes 18874376 | tf_op jit(solution)/shard_map/ppermute | solution.py:368
  5.4 17.5 %collective-permute-start.2 = (bf16[64,4224]{1,0:T(8,128)(2,1)S(1)}, bf16[64,4224]{1,0:T(8,128)(2,1)S(1)}, u32[]{:S(2)}, u32[]{:S(2)}) collective-permute-start(bf16[64,4224]{1,0:T(8,128)(2,1)S(1)} %get-tuple-element.62), channel_id=1, source_target_pairs={{0,2},{1,3},{2,4},{3,5},{4,6},{5,7},{6,0},{7,1},{8,10},{9,11},{10,... | collective-permute-start | bytes 1622024 | tf_op jit(solution)/shard_map/ppermute | solution.py:362
  8.4 9.7 %collective-permute-start = (bf16[336,512]{1,0:T(8,128)(2,1)S(1)}, bf16[336,512]{1,0:T(8,128)(2,1)S(1)}, u32[]{:S(2)}, u32[]{:S(2)}) collective-permute-start(bf16[336,512]{1,0:T(8,128)(2,1)S(1)} %get-tuple-element.59), channel_id=1, source_target_pairs={{0,8},{8,0},{16,24},{24,16},{1,9},{9,1},{17,25},{25,17},{2,10},{10... | collective-permute-start | bytes 1032200 | tf_op jit(solution)/shard_map/ppermute | solution.py:365
  24.6 18.9 %collective-permute-start.6 = (bf16[1,768,4096]{2,1,0:T(8,128)(2,1)S(1)}, bf16[1,768,4096]{2,1,0:T(8,128)(2,1)S(1)}, u32[]{:S(2)}, u32[]{:S(2)}) collective-permute-start(bf16[1,768,4096]{2,1,0:T(8,128)(2,1)S(1)} %bitcast.9), channel_id=1, source_target_pairs={{0,1},{1,0},{2,3},{3,2},{4,5},{5,4},{6,7},{7,6},{8,9},{9,8},{10,11... | collective-permute-start | bytes 18874376 | tf_op jit(solution)/shard_map/ppermute | solution.py:368
  24.6 16.6 %collective-permute-start.7 = (bf16[64,4224]{1,0:T(8,128)(2,1)S(1)}, bf16[64,4224]{1,0:T(8,128)(2,1)}, u32[]{:S(2)}, u32[]{:S(2)}) collective-permute-start(bf16[64,4224]{1,0:T(8,128)(2,1)S(1)} %collective-permute-done.2.wide_ref), channel_id=1, source_target_pairs={{0,2},{1,3},{2,4},{3,5},{4,6},{5,7},{6,0},{7,1},{8,10},{9,11},{10,... | collective-permute-start | bytes 1622024 | tf_op jit(solution)/shard_map/ppermute | solution.py:362
  24.7 16.5 %collective-permute-start.5 = (bf16[336,512]{1,0:T(8,128)(2,1)S(1)}, bf16[336,512]{1,0:T(8,128)(2,1)S(1)}, u32[]{:S(2)}, u32[]{:S(2)}) collective-permute-start(bf16[336,512]{1,0:T(8,128)(2,1)S(1)} %get-tuple-element.64), channel_id=1, source_target_pairs={{0,24},{8,16},{16,8},{24,0},{1,25},{9,17},{17,9},{25,1},{2,26},{10... | collective-permute-start | bytes 1032200 | tf_op jit(solution)/shard_map/ppermute | solution.py:365
  27.2 16.2 %collective-permute-start.8 = (bf16[336,512]{1,0:T(8,128)(2,1)S(1)}, bf16[336,512]{1,0:T(8,128)(2,1)S(1)}, u32[]{:S(2)}, u32[]{:S(2)}) collective-permute-start(bf16[336,512]{1,0:T(8,128)(2,1)S(1)} %get-tuple-element.66), channel_id=1, source_target_pairs={{0,8},{8,0},{16,24},{24,16},{1,9},{9,1},{17,25},{25,17},{2,10},{10... | collective-permute-start | bytes 1032200 | tf_op jit(solution)/shard_map/ppermute | solution.py:365
  27.8 15.7 %collective-permute-start.9 = (bf16[336,512]{1,0:T(8,128)(2,1)S(1)}, bf16[336,512]{1,0:T(8,128)(2,1)S(1)}, u32[]{:S(2)}, u32[]{:S(2)}) collective-permute-start(bf16[336,512]{1,0:T(8,128)(2,1)S(1)} %get-tuple-element.67), channel_id=1, source_target_pairs={{0,16},{8,24},{16,0},{24,8},{1,17},{9,25},{17,1},{25,9},{2,18},{10... | collective-permute-start | bytes 1032200 | tf_op jit(solution)/shard_map/ppermute | solution.py:365
  41.2 27.7 %collective-permute-start.14 = (bf16[64,4224]{1,0:T(8,128)(2,1)}, bf16[64,4224]{1,0:T(8,128)(2,1)}, u32[]{:S(2)}, u32[]{:S(2)}) collective-permute-start(bf16[64,4224]{1,0:T(8,128)(2,1)} %collective-permute-done.7.wide_ref), channel_id=1, source_target_pairs={{0,2},{1,3},{2,4},{3,5},{4,6},{5,7},{6,0},{7,1},{8,10},{9,11},{10,... | collective-permute-start | bytes 1622024 | tf_op jit(solution)/shard_map/ppermute | solution.py:362
  47.0 22.0 %collective-permute-start.10 = (bf16[336,512]{1,0:T(8,128)(2,1)S(1)}, bf16[336,512]{1,0:T(8,128)(2,1)S(1)}, u32[]{:S(2)}, u32[]{:S(2)}) collective-permute-start(bf16[336,512]{1,0:T(8,128)(2,1)S(1)} %get-tuple-element.73), channel_id=1, source_target_pairs={{0,24},{8,16},{16,8},{24,0},{1,25},{9,17},{17,9},{25,1},{2,26},{10... | collective-permute-start | bytes 1032200 | tf_op jit(solution)/shard_map/ppermute | solution.py:365
  49.2 19.8 %collective-permute-start.11 = (bf16[336,512]{1,0:T(8,128)(2,1)S(1)}, bf16[336,512]{1,0:T(8,128)(2,1)S(1)}, u32[]{:S(2)}, u32[]{:S(2)}) collective-permute-start(bf16[336,512]{1,0:T(8,128)(2,1)S(1)} %get-tuple-element.80), channel_id=1, source_target_pairs={{0,8},{8,0},{16,24},{24,16},{1,9},{9,1},{17,25},{25,17},{2,10},{10... | collective-permute-start | bytes 1032200 | tf_op jit(solution)/shard_map/ppermute | solution.py:365
  49.8 19.3 %collective-permute-start.12 = (bf16[336,512]{1,0:T(8,128)(2,1)S(1)}, bf16[336,512]{1,0:T(8,128)(2,1)S(1)}, u32[]{:S(2)}, u32[]{:S(2)}) collective-permute-start(bf16[336,512]{1,0:T(8,128)(2,1)S(1)} %get-tuple-element.81), channel_id=1, source_target_pairs={{0,16},{8,24},{16,0},{24,8},{1,17},{9,25},{17,1},{25,9},{2,18},{10... | collective-permute-start | bytes 1032200 | tf_op jit(solution)/shard_map/ppermute | solution.py:365
  50.5 22.0 %collective-permute-start.13 = (bf16[336,512]{1,0:T(8,128)(2,1)S(1)}, bf16[336,512]{1,0:T(8,128)(2,1)S(1)}, u32[]{:S(2)}, u32[]{:S(2)}) collective-permute-start(bf16[336,512]{1,0:T(8,128)(2,1)S(1)} %get-tuple-element.82), channel_id=1, source_target_pairs={{0,24},{8,16},{16,8},{24,0},{1,25},{9,17},{17,9},{25,1},{2,26},{10... | collective-permute-start | bytes 1032200 | tf_op jit(solution)/shard_map/ppermute | solution.py:365
  76.5 13.9 %collective-permute-start.18 = (bf16[336,512]{1,0:T(8,128)(2,1)S(1)}, bf16[336,512]{1,0:T(8,128)(2,1)S(1)}, u32[]{:S(2)}, u32[]{:S(2)}) collective-permute-start(bf16[336,512]{1,0:T(8,128)(2,1)S(1)} %get-tuple-element.89), channel_id=1, source_target_pairs={{0,8},{8,0},{16,24},{24,16},{1,9},{9,1},{17,25},{25,17},{2,10},{10... | collective-permute-start | bytes 1032200 | tf_op jit(solution)/shard_map/ppermute | solution.py:365
  78.0 15.3 %collective-permute-start.19 = (bf16[336,512]{1,0:T(8,128)(2,1)S(1)}, bf16[336,512]{1,0:T(8,128)(2,1)S(1)}, u32[]{:S(2)}, u32[]{:S(2)}) collective-permute-start(bf16[336,512]{1,0:T(8,128)(2,1)S(1)} %get-tuple-element.90), channel_id=1, source_target_pairs={{0,16},{8,24},{16,0},{24,8},{1,17},{9,25},{17,1},{25,9},{2,18},{10... | collective-permute-start | bytes 1032200 | tf_op jit(solution)/shard_map/ppermute | solution.py:365
  79.5 17.0 %collective-permute-start.20 = (bf16[336,512]{1,0:T(8,128)(2,1)S(1)}, bf16[336,512]{1,0:T(8,128)(2,1)S(1)}, u32[]{:S(2)}, u32[]{:S(2)}) collective-permute-start(bf16[336,512]{1,0:T(8,128)(2,1)S(1)} %get-tuple-element.91), channel_id=1, source_target_pairs={{0,24},{8,16},{16,8},{24,0},{1,25},{9,17},{17,9},{25,1},{2,26},{10... | collective-permute-start | bytes 1032200 | tf_op jit(solution)/shard_map/ppermute | solution.py:365
  91.2 19.7 %collective-permute-start.21 = (bf16[336,512]{1,0:T(8,128)(2,1)}, bf16[336,512]{1,0:T(8,128)(2,1)S(1)}, u32[]{:S(2)}, u32[]{:S(2)}) collective-permute-start(bf16[336,512]{1,0:T(8,128)(2,1)} %get-tuple-element.94), channel_id=1, source_target_pairs={{0,8},{8,0},{16,24},{24,16},{1,9},{9,1},{17,25},{25,17},{2,10},{10... | collective-permute-start | bytes 1032200 | tf_op jit(solution)/shard_map/ppermute | solution.py:365
  94.0 16.9 %collective-permute-start.22 = (bf16[336,512]{1,0:T(8,128)(2,1)}, bf16[336,512]{1,0:T(8,128)(2,1)S(1)}, u32[]{:S(2)}, u32[]{:S(2)}) collective-permute-start(bf16[336,512]{1,0:T(8,128)(2,1)} %get-tuple-element.96), channel_id=1, source_target_pairs={{0,16},{8,24},{16,0},{24,8},{1,17},{9,25},{17,1},{25,9},{2,18},{10... | collective-permute-start | bytes 1032200 | tf_op jit(solution)/shard_map/ppermute | solution.py:365
  97.2 13.7 %collective-permute-start.23 = (bf16[336,512]{1,0:T(8,128)(2,1)}, bf16[336,512]{1,0:T(8,128)(2,1)S(1)}, u32[]{:S(2)}, u32[]{:S(2)}) collective-permute-start(bf16[336,512]{1,0:T(8,128)(2,1)} %get-tuple-element.98), channel_id=1, source_target_pairs={{0,24},{8,16},{16,8},{24,0},{1,25},{9,17},{17,9},{25,1},{2,26},{10... | collective-permute-start | bytes 1032200 | tf_op jit(solution)/shard_map/ppermute | solution.py:365
  107.4 20.9 %collective-permute-start.15 = (bf16[336,512]{1,0:T(8,128)(2,1)}, bf16[336,512]{1,0:T(8,128)(2,1)}, u32[]{:S(2)}, u32[]{:S(2)}) collective-permute-start(bf16[336,512]{1,0:T(8,128)(2,1)} %get-tuple-element.86), channel_id=1, source_target_pairs={{0,8},{8,0},{16,24},{24,16},{1,9},{9,1},{17,25},{25,17},{2,10},{10... | collective-permute-start | bytes 1032200 | tf_op jit(solution)/shard_map/ppermute | solution.py:365
  108.9 21.5 %collective-permute-start.16 = (bf16[336,512]{1,0:T(8,128)(2,1)}, bf16[336,512]{1,0:T(8,128)(2,1)}, u32[]{:S(2)}, u32[]{:S(2)}) collective-permute-start(bf16[336,512]{1,0:T(8,128)(2,1)} %get-tuple-element.87), channel_id=1, source_target_pairs={{0,16},{8,24},{16,0},{24,8},{1,17},{9,25},{17,1},{25,9},{2,18},{10... | collective-permute-start | bytes 1032200 | tf_op jit(solution)/shard_map/ppermute | solution.py:365
  110.9 19.5 %collective-permute-start.17 = (bf16[336,512]{1,0:T(8,128)(2,1)}, bf16[336,512]{1,0:T(8,128)(2,1)}, u32[]{:S(2)}, u32[]{:S(2)}) collective-permute-start(bf16[336,512]{1,0:T(8,128)(2,1)} %get-tuple-element.88), channel_id=1, source_target_pairs={{0,24},{8,16},{16,8},{24,0},{1,25},{9,17},{17,9},{25,1},{2,26},{10... | collective-permute-start | bytes 1032200 | tf_op jit(solution)/shard_map/ppermute | solution.py:365
  114.2 45.6 %collective-permute-start.28 = (bf16[64,4096]{1,0:T(8,128)(2,1)}, bf16[64,4096]{1,0:T(8,128)(2,1)}, u32[]{:S(2)}, u32[]{:S(2)}) collective-permute-start(bf16[64,4096]{1,0:T(8,128)(2,1)} %combine.4.refs_10_), channel_id=1, source_target_pairs={{0,4},{1,5},{2,6},{3,7},{4,0},{5,1},{6,2},{7,3},{8,12},{9,13},{10,... | collective-permute-start | bytes 1572872 | tf_op jit(solution)/shard_map/ppermute | solution.py:362
  126.8 11.2 %collective-permute-start.29 = (bf16[336,512]{1,0:T(8,128)(2,1)}, bf16[336,512]{1,0:T(8,128)(2,1)S(1)}, u32[]{:S(2)}, u32[]{:S(2)}) collective-permute-start(bf16[336,512]{1,0:T(8,128)(2,1)} %get-tuple-element.106), channel_id=1, source_target_pairs={{0,8},{8,0},{16,24},{24,16},{1,9},{9,1},{17,25},{25,17},{2,10},{10... | collective-permute-start | bytes 1032200 | tf_op jit(solution)/shard_map/ppermute | solution.py:365
  128.3 11.2 %collective-permute-start.30 = (bf16[336,512]{1,0:T(8,128)(2,1)}, bf16[336,512]{1,0:T(8,128)(2,1)S(1)}, u32[]{:S(2)}, u32[]{:S(2)}) collective-permute-start(bf16[336,512]{1,0:T(8,128)(2,1)} %get-tuple-element.107), channel_id=1, source_target_pairs={{0,16},{8,24},{16,0},{24,8},{1,17},{9,25},{17,1},{25,9},{2,18},{10... | collective-permute-start | bytes 1032200 | tf_op jit(solution)/shard_map/ppermute | solution.py:365
  130.3 14.7 %collective-permute-start.31 = (bf16[336,512]{1,0:T(8,128)(2,1)}, bf16[336,512]{1,0:T(8,128)(2,1)S(1)}, u32[]{:S(2)}, u32[]{:S(2)}) collective-permute-start(bf16[336,512]{1,0:T(8,128)(2,1)} %get-tuple-element.108), channel_id=1, source_target_pairs={{0,24},{8,16},{16,8},{24,0},{1,25},{9,17},{17,9},{25,1},{2,26},{10... | collective-permute-start | bytes 1032200 | tf_op jit(solution)/shard_map/ppermute | solution.py:365
  133.5 26.2 %collective-permute-start.27 = (bf16[64,4096]{1,0:T(8,128)(2,1)S(1)}, bf16[64,4096]{1,0:T(8,128)(2,1)S(1)}, u32[]{:S(2)}, u32[]{:S(2)}) collective-permute-start(bf16[64,4096]{1,0:T(8,128)(2,1)S(1)} %combine.5.refs_4_), channel_id=1, source_target_pairs={{0,6},{1,7},{2,0},{3,1},{4,2},{5,3},{6,4},{7,5},{8,14},{9,15},{10,... | collective-permute-start | bytes 1572872 | tf_op jit(solution)/shard_map/ppermute | solution.py:362
  138.1 11.6 %collective-permute-start.24 = (bf16[336,512]{1,0:T(8,128)(2,1)S(1)}, bf16[336,512]{1,0:T(8,128)(2,1)S(1)}, u32[]{:S(2)}, u32[]{:S(2)}) collective-permute-start(bf16[336,512]{1,0:T(8,128)(2,1)S(1)} %copy-done.26), channel_id=1, source_target_pairs={{0,8},{8,0},{16,24},{24,16},{1,9},{9,1},{17,25},{25,17},{2,10},{10... | collective-permute-start | bytes 1032200 | tf_op jit(solution)/shard_map/ppermute | solution.py:365
  146.6 13.2 %collective-permute-start.32 = (bf16[64,4096]{1,0:T(8,128)(2,1)S(1)}, bf16[64,4096]{1,0:T(8,128)(2,1)S(1)}, u32[]{:S(2)}, u32[]{:S(2)}) collective-permute-start(bf16[64,4096]{1,0:T(8,128)(2,1)S(1)} %combine.6), channel_id=1, source_target_pairs={{0,2},{1,3},{2,4},{3,5},{4,6},{5,7},{6,0},{7,1},{8,10},{9,11},{10,... | collective-permute-start | bytes 1572872 | tf_op jit(solution)/shard_map/ppermute | solution.py:362
  148.7 11.0 %collective-permute-start.25 = (bf16[336,512]{1,0:T(8,128)(2,1)S(1)}, bf16[336,512]{1,0:T(8,128)(2,1)S(1)}, u32[]{:S(2)}, u32[]{:S(2)}) collective-permute-start(bf16[336,512]{1,0:T(8,128)(2,1)S(1)} %copy-done.25), channel_id=1, source_target_pairs={{0,16},{8,24},{16,0},{24,8},{1,17},{9,25},{17,1},{25,9},{2,18},{10... | collective-permute-start | bytes 1032200 | tf_op jit(solution)/shard_map/ppermute | solution.py:365
  149.6 10.1 %collective-permute-start.26 = (bf16[336,512]{1,0:T(8,128)(2,1)S(1)}, bf16[336,512]{1,0:T(8,128)(2,1)S(1)}, u32[]{:S(2)}, u32[]{:S(2)}) collective-permute-start(bf16[336,512]{1,0:T(8,128)(2,1)S(1)} %copy-done.24), channel_id=1, source_target_pairs={{0,24},{8,16},{16,8},{24,0},{1,25},{9,17},{17,9},{25,1},{2,26},{10... | collective-permute-start | bytes 1032200 | tf_op jit(solution)/shard_map/ppermute | solution.py:365
  (33 other events, 191.3 us)

commit v3 on v2

--- a/solution.py
+++ b/solution.py
@@ -18,7 +18,7 @@
     "F0.3": ["P1"],
     "F1.3": ["P2"],
     "P2": ["F0.3", "F1.1", "F1.2", "S2"],
-    "P3": ["F1.3", "F2.1", "F2.2", "F2.3"],
+    "P3": ["F1.3", "F2.1"],
     "R2.1": ["F3.1"],
     "R2.2": ["F3.2"],
     "R2.3": ["F3.3"],
@@ -29,7 +29,7 @@
 VIA = {}
 F32 = jnp.float32
 BF16 = jnp.bfloat16
-COST = pl.CostEstimate(flops=10**11, transcendentals=0, bytes_accessed=10**8)
+COST = pl.CostEstimate(flops=12 * 10**9, transcendentals=0, bytes_accessed=10**8)
 VMEM = pl.BlockSpec(memory_space=pltpu.VMEM)
 SMEM = pl.BlockSpec(memory_space=pltpu.SMEM)
 ANY = pl.BlockSpec(memory_space=pl.ANY)
@@ -91,6 +91,60 @@
             block[FOLD * main :, :] = ends[:, m * part : (m + 1) * part]
 
 
+def tight(cap, n):
+    main, tail, _ = heights(cap)
+    ends = -(-n * tail // SUB) * SUB
+    return n * main + ends, ends
+
+
+def quotient(value, divisor):
+    return ((value.astype(F32) + 0.5) * (1.0 / divisor)).astype(jnp.int32)
+
+
+def unfold_tight(blocks, cap, rows_ref):
+    main, tail, _ = heights(cap)
+    n, part = len(blocks), blocks[0].shape[1]
+    high, ends = tight(cap, n)
+    if tail:
+        r = iota((FOLD * ends, 1), 0)
+        g = quotient(r, ends)
+        q = r - g * ends
+        m = quotient(q, tail)
+        source = jnp.where(q < n * tail, m * (FOLD * tail) + g * tail + q - m * tail, -1)
+        spread = (iota((FOLD * ends, n * FOLD * tail), 1) == source).astype(BF16)
+        tails = jnp.concatenate([block[FOLD * main :, :] for block in blocks], axis=0)
+        last = jnp.dot(spread, tails, preferred_element_type=F32).astype(BF16)
+    for g in range(FOLD):
+        cols = slice(g * part, (g + 1) * part)
+        if main:
+            for m, block in enumerate(blocks):
+                rows_ref[m * main : (m + 1) * main, cols] = block[g * main : (g + 1) * main, :]
+        if tail:
+            rows_ref[high - ends : high, cols] = last[g * ends : (g + 1) * ends]
+
+
+def fold_tight(rows_ref, cap, blocks):
+    main, tail, _ = heights(cap)
+    n, part = len(blocks), blocks[0].shape[1]
+    high, ends = tight(cap, n)
+    columns = [slice(g * part, (g + 1) * part) for g in range(FOLD)]
+    if tail:
+        r = iota((n * FOLD * tail, 1), 0)
+        m = quotient(r, FOLD * tail)
+        rest = r - m * (FOLD * tail)
+        g = quotient(rest, tail)
+        source = g * ends + m * tail + rest - g * tail
+        gather = (iota((n * FOLD * tail, FOLD * ends), 1) == source).astype(BF16)
+        last = jnp.concatenate([rows_ref[high - ends : high, cols] for cols in columns], axis=0)
+        tails = jnp.dot(gather, last, preferred_element_type=F32).astype(BF16)
+    for m, block in enumerate(blocks):
+        if main:
+            for g, cols in enumerate(columns):
+                block[g * main : (g + 1) * main, :] = rows_ref[m * main : (m + 1) * main, cols]
+        if tail:
+            block[FOLD * main :, :] = tails[m * FOLD * tail : (m + 1) * FOLD * tail]
+
+
 def slot_codes(weights):
     rows = weights.shape[0]
     named = weights > 0.0
@@ -170,7 +224,7 @@
         cost_estimate=COST,
         compiler_params=pltpu.CompilerParams(vmem_limit_bytes=12 << 20),
         name="first",
-    )(ids, x, routes.T, gate_fixed.T)
+    )(ids, *[pltpu.with_memory_space_constraint(a, pltpu.HBM) for a in (x, routes.T, gate_fixed.T)])
 
 
 def pack_kernel(n, cap, ids_ref, wide_ref, *refs):
@@ -203,7 +257,7 @@
 
 def expert_body(cap, blocks, weights, outs, x_ref, h_ref, y_ref, ready):
     half, width = weights[2].shape[1:]
-    unfold(blocks, cap, x_ref)
+    unfold_tight(blocks, cap, x_ref)
     x = x_ref[...]
     steps = expert_steps(half, width)
     for i, (s, j) in enumerate(steps):
@@ -224,7 +278,7 @@
                 for t in range(2)
             )
             y_ref[:, j : j + 2 * TILE] = total.astype(BF16)
-    fold(y_ref, cap, outs)
+    fold_tight(y_ref, cap, outs)
 
 
 def expert_steps(half, width):
@@ -275,7 +329,7 @@
 def expert(blocks, weights, cap, after=(), first_call=False):
     n = len(blocks)
     half, width = weights[2].shape[1:]
-    rows = n * heights(cap)[2]
+    rows = tight(cap, n)[0]
     out_shape = tuple(jax.ShapeDtypeStruct(b.shape, b.dtype) for b in blocks)
     scratch = [
         pltpu.VMEM((rows, width), BF16),

time: 163 us -> 155 us (0.951)
  Pallas kernels: 64.2 us -> 59.5 us
  local copies, waits for them, and re-layouts: 10.1 us -> 6.67 us
    unnamed x64 -> x60, local copies, waits for them, and re-layouts: 10.1 us -> 6.67 us
    pallas_call x4, Pallas kernels: 8.94 us -> 6.93 us  [combine(): pl.pallas_call(functools.partial(combine_kernel, n, len(others), cap), ou...]
    pallas_call x4, Pallas kernels: 47.3 us -> 45.5 us  [expert(): pl.pallas_call(functools.partial(kernel, n, cap), out_shape=out_shape, in...]
  transfers between devices with their start and end apart: 33 -> 33, of which waited for: 11 -> 11; matrix products, arithmetic and copies ran while one was open for 0% -> 0% of each run, Pallas kernels for 35% -> 36%
where the time goes in v3:
time: 155 us
  Pallas kernels  59.5 us (38%)
  waiting for transfers between devices  46.2 us (30%)
  starting transfers between devices  41.8 us (27%)
  local copies, waits for them, and re-layouts  6.67 us (4%)
    pallas_call x4, Pallas kernels, expert(): pl.pallas_call(functools.partial(kernel, n, cap), out_shape=out_shape, in...  45.5 us
    ppermute x24, starting transfers between devices, across(): return lax.ppermute(block, 'dp', [(i, i ^ m) for i in range(n_data)])  31.4 us
    ppermute x24, waiting for transfers between devices, across(): return lax.ppermute(block, 'dp', [(i, i ^ m) for i in range(n_data)])  31.3 us
    ppermute x6, waiting for transfers between devices, along(): return lax.ppermute(block, 'expert', pairs)  14.9 us
    ppermute x6, starting transfers between devices, along(): return lax.ppermute(block, 'expert', pairs)  9.83 us
    pallas_call x4, Pallas kernels, combine(): pl.pallas_call(functools.partial(combine_kernel, n, len(others), cap), ou...  6.93 us
    unnamed x60, local copies, waits for them, and re-layouts  6.67 us
    pallas_call x3, Pallas kernels, pack(): pl.pallas_call(functools.partial(pack_kernel, n, cap), out_shape=(jax.Sha...  4.88 us
  transfers between devices with their start and end apart: 33, of which 11 were waited for; matrix products, arithmetic and copies ran while one was open for 0% of the time, Pallas kernels for 36%

profile of v3, /device:TPU:0, one launch (start us, length us, event | category | flops | bytes accessed | tf_op | source)
XLA Modules:
  0.0 154.6 jit_solution(1084926562510259254)
XLA Ops:
  0.6 2.2 %first.1 = (f32[64,16]{1,0:T(8,128)S(1)}, bf16[64,4224]{1,0:T(8,128)(2,1)S(1)}, bf16[336,512]{1,0:T(8,128)(2,1)S(1)}, bf16[336,512]{1,0:T(8,128)(2,1)S(1)}, bf16...) custom-call(s32[4]{0:T(128)S(1)} %pad_add_fusion.ids_ref, bf16[64,4096]{1,0:T(8,128)(2,1)} %x_ref.1, ...), custom_call_target="tpu_custom_call" | custom-call | flops 12000000000 | bytes 100000000 | tf_op jit(solution)/shard_map/first/pallas_call | solution.py:214
  2.8 3.1 %collective-permute-start.2 = (bf16[64,4224]{1,0:T(8,128)(2,1)S(1)}, bf16[64,4224]{1,0:T(8,128)(2,1)S(1)}, u32[]{:S(2)}, u32[]{:S(2)}) collective-permute-start(bf16[64,4224]{1,0:T(8,128)(2,1)S(1)} %get-tuple-element.62), channel_id=1, source_target_pairs={{0,2},{1,3},{2,4},{3,5},{4,6},{5,7},{6,0},{7,1},{8,10},{9,11},{10,... | collective-permute-start | bytes 1622024 | tf_op jit(solution)/shard_map/ppermute | solution.py:416
  5.9 1.5 collective-permute-start
  7.3 1.5 collective-permute-start.1
  8.9 6.7 %collective-permute-done.refs_0_.refs_1_ = bf16[336,512]{1,0:T(8,128)(2,1)S(1)} collective-permute-done((bf16[336,512]{1,0:T(8,128)(2,1)S(1)}, bf16[336,512]{1,0:T(8,128)(2,1)S(1)}, u32[]{:S(2)}, u32[]{:S(2)}) %collective-permute-start) | collective-permute-done | bytes 344096 | tf_op jit(solution)/shard_map/ppermute | solution.py:419
  16.8 3.6 %collective-permute-done.2.wide_ref = bf16[64,4224]{1,0:T(8,128)(2,1)S(1)} collective-permute-done((bf16[64,4224]{1,0:T(8,128)(2,1)S(1)}, bf16[64,4224]{1,0:T(8,128)(2,1)S(1)}, u32[]{:S(2)}, u32[]{:S(2)}) %collective-permute-start.2) | collective-permute-done | bytes 540704 | tf_op jit(solution)/shard_map/ppermute | solution.py:416
  20.3 1.6 %pack.3 = (f32[64,16]{1,0:T(8,128)S(1)}, bf16[336,512]{1,0:T(8,128)(2,1)S(1)}, bf16[336,512]{1,0:T(8,128)(2,1)S(1)}, bf16[336,512]{1,0:T(8,128)(2,1)S(1)}, bf16[336,512]{1,0:T(8,128)(2,1)S(1)}) custom-call(s32[4]{0:T(128)S(1)} %pad_add_fusion.ids_ref, bf16[64,4224]{1,0:T(8,128)(2,1)S(1)} %collective-permute-done.2.wide_ref, ...), custom_call_target="tpu_custom_call" | custom-call | flops 12000000000 | bytes 100000000 | tf_op jit(solution)/shard_map/pack/pallas_call | solution.py:246
  22.1 2.3 %collective-permute-start.7 = (bf16[64,4224]{1,0:T(8,128)(2,1)S(1)}, bf16[64,4224]{1,0:T(8,128)(2,1)S(1)}, u32[]{:S(2)}, u32[]{:S(2)}) collective-permute-start(bf16[64,4224]{1,0:T(8,128)(2,1)S(1)} %collective-permute-done.2.wide_ref), channel_id=1, source_target_pairs={{0,2},{1,3},{2,4},{3,5},{4,6},{5,7},{6,0},{7,1},{8,10},{9,11},{10,... | collective-permute-start | bytes 1622024 | tf_op jit(solution)/shard_map/ppermute | solution.py:416
  24.4 2.4 %collective-permute-start.5 = (bf16[336,512]{1,0:T(8,128)(2,1)S(1)}, bf16[336,512]{1,0:T(8,128)(2,1)S(1)}, u32[]{:S(2)}, u32[]{:S(2)}) collective-permute-start(bf16[336,512]{1,0:T(8,128)(2,1)S(1)} %get-tuple-element.64), channel_id=1, source_target_pairs={{0,24},{8,16},{16,8},{24,0},{1,25},{9,17},{17,9},{25,1},{2,26},{10... | collective-permute-start | bytes 1032200 | tf_op jit(solution)/shard_map/ppermute | solution.py:419
  27.9 11.3 %collective-permute-done.7.wide_ref = bf16[64,4224]{1,0:T(8,128)(2,1)S(1)} collective-permute-done((bf16[64,4224]{1,0:T(8,128)(2,1)S(1)}, bf16[64,4224]{1,0:T(8,128)(2,1)S(1)}, u32[]{:S(2)}, u32[]{:S(2)}) %collective-permute-start.7) | collective-permute-done | bytes 540704 | tf_op jit(solution)/shard_map/ppermute | solution.py:416
  39.3 3.6 %collective-permute-done.8.refs_2_.refs_1_ = bf16[336,512]{1,0:T(8,128)(2,1)S(1)} collective-permute-done((bf16[336,512]{1,0:T(8,128)(2,1)S(1)}, bf16[336,512]{1,0:T(8,128)(2,1)S(1)}, u32[]{:S(2)}, u32[]{:S(2)}) %collective-permute-start.8) | collective-permute-done | bytes 344096 | tf_op jit(solution)/shard_map/ppermute | solution.py:419
  42.9 1.6 %pack.4 = (f32[64,16]{1,0:T(8,128)S(1)}, bf16[336,512]{1,0:T(8,128)(2,1)S(1)}, bf16[336,512]{1,0:T(8,128)(2,1)S(1)}, bf16[336,512]{1,0:T(8,128)(2,1)S(1)}, bf16[336,512]{1,0:T(8,128)(2,1)S(1)}) custom-call(s32[4]{0:T(128)S(1)} %pad_add_fusion.ids_ref, bf16[64,4224]{1,0:T(8,128)(2,1)S(1)} %collective-permute-done.7.wide_ref, ...), custom_call_target="tpu_custom_call" | custom-call | flops 12000000000 | bytes 100000000 | tf_op jit(solution)/shard_map/pack/pallas_call | solution.py:246
  46.4 2.2 %collective-permute-start.10 = (bf16[336,512]{1,0:T(8,128)(2,1)S(1)}, bf16[336,512]{1,0:T(8,128)(2,1)S(1)}, u32[]{:S(2)}, u32[]{:S(2)}) collective-permute-start(bf16[336,512]{1,0:T(8,128)(2,1)S(1)} %get-tuple-element.73), channel_id=1, source_target_pairs={{0,24},{8,16},{16,8},{24,0},{1,25},{9,17},{17,9},{25,1},{2,26},{10... | collective-permute-start | bytes 1032200 | tf_op jit(solution)/shard_map/ppermute | solution.py:419
  49.9 2.2 %collective-permute-start.13 = (bf16[336,512]{1,0:T(8,128)(2,1)S(1)}, bf16[336,512]{1,0:T(8,128)(2,1)S(1)}, u32[]{:S(2)}, u32[]{:S(2)}) collective-permute-start(bf16[336,512]{1,0:T(8,128)(2,1)S(1)} %get-tuple-element.82), channel_id=1, source_target_pairs={{0,24},{8,16},{16,8},{24,0},{1,25},{9,17},{17,9},{25,1},{2,26},{10... | collective-permute-start | bytes 1032200 | tf_op jit(solution)/shard_map/ppermute | solution.py:419
  52.1 15.9 %expert_first.1 = (bf16[336,512]{1,0:T(8,128)(2,1)}, bf16[336,512]{1,0:T(8,128)(2,1)}, bf16[336,512]{1,0:T(8,128)(2,1)}, bf16[336,512]{1,0:T(8,128)(2,1)}, bf16[...) custom-call(bf16[336,512]{1,0:T(8,128)(2,1)} %copy-done.15, ...), custom_call_target="tpu_custom_call" | custom-call | flops 12000000000 | bytes 100000000 | tf_op jit(solution)/shard_map/expert_first/pallas_call | solution.py:346
  69.3 1.6 %pack.5 = (f32[64,16]{1,0:T(8,128)S(1)}, bf16[336,512]{1,0:T(8,128)(2,1)S(1)}, bf16[336,512]{1,0:T(8,128)(2,1)S(1)}, bf16[336,512]{1,0:T(8,128)(2,1)S(1)}, bf16[336,512]{1,0:T(8,128)(2,1)S(1)}) custom-call(s32[4]{0:T(128)S(1)} %pad_add_fusion.ids_ref, bf16[64,4224]{1,0:T(8,128)(2,1)S(1)} %collective-permute-done.14.wide_ref, ...), custom_call_target="tpu_custom_call" | custom-call | flops 12000000000 | bytes 100000000 | tf_op jit(solution)/shard_map/pack/pallas_call | solution.py:246
  73.0 2.2 %collective-permute-start.20 = (bf16[336,512]{1,0:T(8,128)(2,1)S(1)}, bf16[336,512]{1,0:T(8,128)(2,1)S(1)}, u32[]{:S(2)}, u32[]{:S(2)}) collective-permute-start(bf16[336,512]{1,0:T(8,128)(2,1)S(1)} %get-tuple-element.91), channel_id=1, source_target_pairs={{0,24},{8,16},{16,8},{24,0},{1,25},{9,17},{17,9},{25,1},{2,26},{10... | collective-permute-start | bytes 1032200 | tf_op jit(solution)/shard_map/ppermute | solution.py:419
  76.1 9.9 %expert.3 = (bf16[336,512]{1,0:T(8,128)(2,1)}, bf16[336,512]{1,0:T(8,128)(2,1)}, bf16[336,512]{1,0:T(8,128)(2,1)}, bf16[336,512]{1,0:T(8,128)(2,1)}) custom-call(bf16[336,512]{1,0:T(8,128)(2,1)} %copy-done.18, bf16[336,512]{1,0:T(8,128)(2,1)} %copy-done.7, bf16[336,512]{1,0:T(8,128)(2,1)} %copy-done.26, bf16[336,512]{1,0:T(8,128)(2,1)} %copy-done.27, ...), custom_call_target="tpu_custom_call" | custom-call | flops 12000000000 | bytes 100000000 | tf_op jit(solution)/shard_map/expert/pallas_call | solution.py:346
  89.0 2.8 %collective-permute-start.23 = (bf16[336,512]{1,0:T(8,128)(2,1)}, bf16[336,512]{1,0:T(8,128)(2,1)S(1)}, u32[]{:S(2)}, u32[]{:S(2)}) collective-permute-start(bf16[336,512]{1,0:T(8,128)(2,1)} %get-tuple-element.98), channel_id=1, source_target_pairs={{0,24},{8,16},{16,8},{24,0},{1,25},{9,17},{17,9},{25,1},{2,26},{10... | collective-permute-start | bytes 1032200 | tf_op jit(solution)/shard_map/ppermute | solution.py:419
  91.7 9.7 %expert.4 = (bf16[336,512]{1,0:T(8,128)(2,1)}, bf16[336,512]{1,0:T(8,128)(2,1)}, bf16[336,512]{1,0:T(8,128)(2,1)}, bf16[336,512]{1,0:T(8,128)(2,1)}) custom-call(bf16[336,512]{1,0:T(8,128)(2,1)} %copy-done.14, bf16[336,512]{1,0:T(8,128)(2,1)} %copy-done.2, bf16[336,512]{1,0:T(8,128)(2,1)} %copy-done.3, bf16[336,512]{1,0:T(8,128)(2,1)} %copy-done.4, ...), custom_call_target="tpu_custom_call" | custom-call | flops 12000000000 | bytes 100000000 | tf_op jit(solution)/shard_map/expert/pallas_call | solution.py:346
  102.3 2.8 %collective-permute-start.17 = (bf16[336,512]{1,0:T(8,128)(2,1)}, bf16[336,512]{1,0:T(8,128)(2,1)S(1)}, u32[]{:S(2)}, u32[]{:S(2)}) collective-permute-start(bf16[336,512]{1,0:T(8,128)(2,1)} %get-tuple-element.88), channel_id=1, source_target_pairs={{0,24},{8,16},{16,8},{24,0},{1,25},{9,17},{17,9},{25,1},{2,26},{10... | collective-permute-start | bytes 1032200 | tf_op jit(solution)/shard_map/ppermute | solution.py:419
  106.0 1.5 combine.4.refs_10_
  107.5 2.6 %collective-permute-start.28 = (bf16[64,4096]{1,0:T(8,128)(2,1)S(1)}, bf16[64,4096]{1,0:T(8,128)(2,1)S(1)}, u32[]{:S(2)}, u32[]{:S(2)}) collective-permute-start(bf16[64,4096]{1,0:T(8,128)(2,1)S(1)} %combine.4.refs_10_), channel_id=1, source_target_pairs={{0,4},{1,5},{2,6},{3,7},{4,0},{5,1},{6,2},{7,3},{8,12},{9,13},{10,... | collective-permute-start | bytes 1572872 | tf_op jit(solution)/shard_map/ppermute | solution.py:416
  110.2 10.0 %expert.5 = (bf16[336,512]{1,0:T(8,128)(2,1)}, bf16[336,512]{1,0:T(8,128)(2,1)}, bf16[336,512]{1,0:T(8,128)(2,1)}, bf16[336,512]{1,0:T(8,128)(2,1)}) custom-call(bf16[336,512]{1,0:T(8,128)(2,1)} %copy-done.9, bf16[336,512]{1,0:T(8,128)(2,1)} %copy-done.23, bf16[336,512]{1,0:T(8,128)(2,1)} %copy-done.24, bf16[336,512]{1,0:T(8,128)(2,1)} %copy-done.25, ...), custom_call_target="tpu_custom_call" | custom-call | flops 12000000000 | bytes 100000000 | tf_op jit(solution)/shard_map/expert/pallas_call | solution.py:346
  121.8 1.8 %collective-permute-start.31 = (bf16[336,512]{1,0:T(8,128)(2,1)}, bf16[336,512]{1,0:T(8,128)(2,1)S(1)}, u32[]{:S(2)}, u32[]{:S(2)}) collective-permute-start(bf16[336,512]{1,0:T(8,128)(2,1)} %get-tuple-element.108), channel_id=1, source_target_pairs={{0,24},{8,16},{16,8},{24,0},{1,25},{9,17},{17,9},{25,1},{2,26},{10... | collective-permute-start | bytes 1032200 | tf_op jit(solution)/shard_map/ppermute | solution.py:419
  124.6 1.5 combine.5.refs_4_
  127.5 3.8 %collective-permute-done.29.refs_1_ = bf16[336,512]{1,0:T(8,128)(2,1)S(1)} collective-permute-done((bf16[336,512]{1,0:T(8,128)(2,1)}, bf16[336,512]{1,0:T(8,128)(2,1)S(1)}, u32[]{:S(2)}, u32[]{:S(2)}) %collective-permute-start.29) | collective-permute-done | bytes 344096 | tf_op jit(solution)/shard_map/ppermute | solution.py:419
  132.8 5.2 %collective-permute-done.31.refs_3_ = bf16[336,512]{1,0:T(8,128)(2,1)S(1)} collective-permute-done((bf16[336,512]{1,0:T(8,128)(2,1)}, bf16[336,512]{1,0:T(8,128)(2,1)S(1)}, u32[]{:S(2)}, u32[]{:S(2)}) %collective-permute-start.31) | collective-permute-done | bytes 344096 | tf_op jit(solution)/shard_map/ppermute | solution.py:419
  138.0 1.5 combine.6
  142.0 3.1 %collective-permute-start.26 = (bf16[336,512]{1,0:T(8,128)(2,1)S(1)}, bf16[336,512]{1,0:T(8,128)(2,1)S(1)}, u32[]{:S(2)}, u32[]{:S(2)}) collective-permute-start(bf16[336,512]{1,0:T(8,128)(2,1)S(1)} %copy-done.20), channel_id=1, source_target_pairs={{0,24},{8,16},{16,8},{24,0},{1,25},{9,17},{17,9},{25,1},{2,26},{10... | collective-permute-start | bytes 1032200 | tf_op jit(solution)/shard_map/ppermute | solution.py:419
  145.1 7.1 %collective-permute-done.25.refs_2_ = bf16[336,512]{1,0:T(8,128)(2,1)S(1)} collective-permute-done((bf16[336,512]{1,0:T(8,128)(2,1)S(1)}, bf16[336,512]{1,0:T(8,128)(2,1)S(1)}, u32[]{:S(2)}, u32[]{:S(2)}) %collective-permute-start.25) | collective-permute-done | bytes 344096 | tf_op jit(solution)/shard_map/ppermute | solution.py:419
  152.1 2.5 %combine.7 = bf16[64,4096]{1,0:T(8,128)(2,1)} custom-call(s32[4]{0:T(128)S(1)} %pad_add_fusion.ids_ref, f32[64,16]{1,0:T(8,128)S(1)} %get-tuple-element.57.w_ref, bf16[336,512]{1,0:T(8,128)(2,1)S(1)} %copy-done.13, bf16[336,512]{1,0:T(8,128)(2,1)S(1)} %collective-permute-done.24.refs_1_, bf16[336,512]{1,0:T(8,128)(2,1)S(1)} %collective-permute-done.25.refs_2_, ...), custom_call_target="tpu_custom_call" | custom-call | flops 12000000000 | bytes 100000000 | tf_op jit(solution)/shard_map/combine/pallas_call | solution.py:382
  (108 shorter events, 23.0 us)
Async XLA Ops:
  0.0 20.3 %collective-permute-start.3 = (bf16[1,4096,768]{2,1,0:T(8,128)(2,1)}, bf16[1,4096,768]{2,1,0:T(8,128)(2,1)}, u32[]{:S(2)}, u32[]{:S(2)}) collective-permute-start(bf16[1,4096,768]{2,1,0:T(8,128)(2,1)} %refs_4_.1), channel_id=1, source_target_pairs={{0,1},{1,0},{2,3},{3,2},{4,5},{5,4},{6,7},{7,6},{8,9},{9,8},{10,11... | collective-permute-start | bytes 18874376 | tf_op jit(solution)/shard_map/ppermute | solution.py:422
  0.5 19.9 %collective-permute-start.4 = (bf16[1,4096,768]{2,1,0:T(8,128)(2,1)}, bf16[1,4096,768]{2,1,0:T(8,128)(2,1)}, u32[]{:S(2)}, u32[]{:S(2)}) collective-permute-start(bf16[1,4096,768]{2,1,0:T(8,128)(2,1)} %refs_5_.1), channel_id=1, source_target_pairs={{0,1},{1,0},{2,3},{3,2},{4,5},{5,4},{6,7},{7,6},{8,9},{9,8},{10,11... | collective-permute-start | bytes 18874376 | tf_op jit(solution)/shard_map/ppermute | solution.py:422
  2.8 17.5 %collective-permute-start.2 = (bf16[64,4224]{1,0:T(8,128)(2,1)S(1)}, bf16[64,4224]{1,0:T(8,128)(2,1)S(1)}, u32[]{:S(2)}, u32[]{:S(2)}) collective-permute-start(bf16[64,4224]{1,0:T(8,128)(2,1)S(1)} %get-tuple-element.62), channel_id=1, source_target_pairs={{0,2},{1,3},{2,4},{3,5},{4,6},{5,7},{6,0},{7,1},{8,10},{9,11},{10,... | collective-permute-start | bytes 1622024 | tf_op jit(solution)/shard_map/ppermute | solution.py:416
  5.9 9.7 %collective-permute-start = (bf16[336,512]{1,0:T(8,128)(2,1)S(1)}, bf16[336,512]{1,0:T(8,128)(2,1)S(1)}, u32[]{:S(2)}, u32[]{:S(2)}) collective-permute-start(bf16[336,512]{1,0:T(8,128)(2,1)S(1)} %get-tuple-element.59), channel_id=1, source_target_pairs={{0,8},{8,0},{16,24},{24,16},{1,9},{9,1},{17,25},{25,17},{2,10},{10... | collective-permute-start | bytes 1032200 | tf_op jit(solution)/shard_map/ppermute | solution.py:419
  22.0 20.8 %collective-permute-start.6 = (bf16[1,768,4096]{2,1,0:T(8,128)(2,1)S(1)}, bf16[1,768,4096]{2,1,0:T(8,128)(2,1)S(1)}, u32[]{:S(2)}, u32[]{:S(2)}) collective-permute-start(bf16[1,768,4096]{2,1,0:T(8,128)(2,1)S(1)} %bitcast.7), channel_id=1, source_target_pairs={{0,1},{1,0},{2,3},{3,2},{4,5},{5,4},{6,7},{7,6},{8,9},{9,8},{10,11... | collective-permute-start | bytes 18874376 | tf_op jit(solution)/shard_map/ppermute | solution.py:422
  22.1 17.2 %collective-permute-start.7 = (bf16[64,4224]{1,0:T(8,128)(2,1)S(1)}, bf16[64,4224]{1,0:T(8,128)(2,1)S(1)}, u32[]{:S(2)}, u32[]{:S(2)}) collective-permute-start(bf16[64,4224]{1,0:T(8,128)(2,1)S(1)} %collective-permute-done.2.wide_ref), channel_id=1, source_target_pairs={{0,2},{1,3},{2,4},{3,5},{4,6},{5,7},{6,0},{7,1},{8,10},{9,11},{10,... | collective-permute-start | bytes 1622024 | tf_op jit(solution)/shard_map/ppermute | solution.py:416
  24.4 14.8 %collective-permute-start.5 = (bf16[336,512]{1,0:T(8,128)(2,1)S(1)}, bf16[336,512]{1,0:T(8,128)(2,1)S(1)}, u32[]{:S(2)}, u32[]{:S(2)}) collective-permute-start(bf16[336,512]{1,0:T(8,128)(2,1)S(1)} %get-tuple-element.64), channel_id=1, source_target_pairs={{0,24},{8,16},{16,8},{24,0},{1,25},{9,17},{17,9},{25,1},{2,26},{10... | collective-permute-start | bytes 1032200 | tf_op jit(solution)/shard_map/ppermute | solution.py:419
  26.9 16.0 %collective-permute-start.8 = (bf16[336,512]{1,0:T(8,128)(2,1)S(1)}, bf16[336,512]{1,0:T(8,128)(2,1)S(1)}, u32[]{:S(2)}, u32[]{:S(2)}) collective-permute-start(bf16[336,512]{1,0:T(8,128)(2,1)S(1)} %get-tuple-element.66), channel_id=1, source_target_pairs={{0,8},{8,0},{16,24},{24,16},{1,9},{9,1},{17,25},{25,17},{2,10},{10... | collective-permute-start | bytes 1032200 | tf_op jit(solution)/shard_map/ppermute | solution.py:419
  27.4 15.4 %collective-permute-start.9 = (bf16[336,512]{1,0:T(8,128)(2,1)S(1)}, bf16[336,512]{1,0:T(8,128)(2,1)S(1)}, u32[]{:S(2)}, u32[]{:S(2)}) collective-permute-start(bf16[336,512]{1,0:T(8,128)(2,1)S(1)} %get-tuple-element.67), channel_id=1, source_target_pairs={{0,16},{8,24},{16,0},{24,8},{1,17},{9,25},{17,1},{25,9},{2,18},{10... | collective-permute-start | bytes 1032200 | tf_op jit(solution)/shard_map/ppermute | solution.py:419
  39.3 28.8 %collective-permute-start.14 = (bf16[64,4224]{1,0:T(8,128)(2,1)S(1)}, bf16[64,4224]{1,0:T(8,128)(2,1)S(1)}, u32[]{:S(2)}, u32[]{:S(2)}) collective-permute-start(bf16[64,4224]{1,0:T(8,128)(2,1)S(1)} %collective-permute-done.7.wide_ref), channel_id=1, source_target_pairs={{0,2},{1,3},{2,4},{3,5},{4,6},{5,7},{6,0},{7,1},{8,10},{9,11},{10,... | collective-permute-start | bytes 1622024 | tf_op jit(solution)/shard_map/ppermute | solution.py:416
  46.4 21.7 %collective-permute-start.10 = (bf16[336,512]{1,0:T(8,128)(2,1)S(1)}, bf16[336,512]{1,0:T(8,128)(2,1)S(1)}, u32[]{:S(2)}, u32[]{:S(2)}) collective-permute-start(bf16[336,512]{1,0:T(8,128)(2,1)S(1)} %get-tuple-element.73), channel_id=1, source_target_pairs={{0,24},{8,16},{16,8},{24,0},{1,25},{9,17},{17,9},{25,1},{2,26},{10... | collective-permute-start | bytes 1032200 | tf_op jit(solution)/shard_map/ppermute | solution.py:419
  48.6 19.5 %collective-permute-start.11 = (bf16[336,512]{1,0:T(8,128)(2,1)S(1)}, bf16[336,512]{1,0:T(8,128)(2,1)S(1)}, u32[]{:S(2)}, u32[]{:S(2)}) collective-permute-start(bf16[336,512]{1,0:T(8,128)(2,1)S(1)} %get-tuple-element.80), channel_id=1, source_target_pairs={{0,8},{8,0},{16,24},{24,16},{1,9},{9,1},{17,25},{25,17},{2,10},{10... | collective-permute-start | bytes 1032200 | tf_op jit(solution)/shard_map/ppermute | solution.py:419
  49.2 26.1 %collective-permute-start.12 = (bf16[336,512]{1,0:T(8,128)(2,1)S(1)}, bf16[336,512]{1,0:T(8,128)(2,1)S(1)}, u32[]{:S(2)}, u32[]{:S(2)}) collective-permute-start(bf16[336,512]{1,0:T(8,128)(2,1)S(1)} %get-tuple-element.81), channel_id=1, source_target_pairs={{0,16},{8,24},{16,0},{24,8},{1,17},{9,25},{17,1},{25,9},{2,18},{10... | collective-permute-start | bytes 1032200 | tf_op jit(solution)/shard_map/ppermute | solution.py:419
  49.9 25.4 %collective-permute-start.13 = (bf16[336,512]{1,0:T(8,128)(2,1)S(1)}, bf16[336,512]{1,0:T(8,128)(2,1)S(1)}, u32[]{:S(2)}, u32[]{:S(2)}) collective-permute-start(bf16[336,512]{1,0:T(8,128)(2,1)S(1)} %get-tuple-element.82), channel_id=1, source_target_pairs={{0,24},{8,16},{16,8},{24,0},{1,25},{9,17},{17,9},{25,1},{2,26},{10... | collective-permute-start | bytes 1032200 | tf_op jit(solution)/shard_map/ppermute | solution.py:419
  71.7 14.3 %collective-permute-start.18 = (bf16[336,512]{1,0:T(8,128)(2,1)S(1)}, bf16[336,512]{1,0:T(8,128)(2,1)S(1)}, u32[]{:S(2)}, u32[]{:S(2)}) collective-permute-start(bf16[336,512]{1,0:T(8,128)(2,1)S(1)} %get-tuple-element.89), channel_id=1, source_target_pairs={{0,8},{8,0},{16,24},{24,16},{1,9},{9,1},{17,25},{25,17},{2,10},{10... | collective-permute-start | bytes 1032200 | tf_op jit(solution)/shard_map/ppermute | solution.py:419
  72.3 15.3 %collective-permute-start.19 = (bf16[336,512]{1,0:T(8,128)(2,1)S(1)}, bf16[336,512]{1,0:T(8,128)(2,1)S(1)}, u32[]{:S(2)}, u32[]{:S(2)}) collective-permute-start(bf16[336,512]{1,0:T(8,128)(2,1)S(1)} %get-tuple-element.90), channel_id=1, source_target_pairs={{0,16},{8,24},{16,0},{24,8},{1,17},{9,25},{17,1},{25,9},{2,18},{10... | collective-permute-start | bytes 1032200 | tf_op jit(solution)/shard_map/ppermute | solution.py:419
  73.0 16.0 %collective-permute-start.20 = (bf16[336,512]{1,0:T(8,128)(2,1)S(1)}, bf16[336,512]{1,0:T(8,128)(2,1)S(1)}, u32[]{:S(2)}, u32[]{:S(2)}) collective-permute-start(bf16[336,512]{1,0:T(8,128)(2,1)S(1)} %get-tuple-element.91), channel_id=1, source_target_pairs={{0,24},{8,16},{16,8},{24,0},{1,25},{9,17},{17,9},{25,1},{2,26},{10... | collective-permute-start | bytes 1032200 | tf_op jit(solution)/shard_map/ppermute | solution.py:419
  86.0 16.3 %collective-permute-start.21 = (bf16[336,512]{1,0:T(8,128)(2,1)}, bf16[336,512]{1,0:T(8,128)(2,1)S(1)}, u32[]{:S(2)}, u32[]{:S(2)}) collective-permute-start(bf16[336,512]{1,0:T(8,128)(2,1)} %get-tuple-element.94), channel_id=1, source_target_pairs={{0,8},{8,0},{16,24},{24,16},{1,9},{9,1},{17,25},{25,17},{2,10},{10... | collective-permute-start | bytes 1032200 | tf_op jit(solution)/shard_map/ppermute | solution.py:419
  87.6 17.4 %collective-permute-start.22 = (bf16[336,512]{1,0:T(8,128)(2,1)}, bf16[336,512]{1,0:T(8,128)(2,1)S(1)}, u32[]{:S(2)}, u32[]{:S(2)}) collective-permute-start(bf16[336,512]{1,0:T(8,128)(2,1)} %get-tuple-element.96), channel_id=1, source_target_pairs={{0,16},{8,24},{16,0},{24,8},{1,17},{9,25},{17,1},{25,9},{2,18},{10... | collective-permute-start | bytes 1032200 | tf_op jit(solution)/shard_map/ppermute | solution.py:419
  89.0 16.1 %collective-permute-start.23 = (bf16[336,512]{1,0:T(8,128)(2,1)}, bf16[336,512]{1,0:T(8,128)(2,1)S(1)}, u32[]{:S(2)}, u32[]{:S(2)}) collective-permute-start(bf16[336,512]{1,0:T(8,128)(2,1)} %get-tuple-element.98), channel_id=1, source_target_pairs={{0,24},{8,16},{16,8},{24,0},{1,25},{9,17},{17,9},{25,1},{2,26},{10... | collective-permute-start | bytes 1032200 | tf_op jit(solution)/shard_map/ppermute | solution.py:419
  101.5 20.1 %collective-permute-start.15 = (bf16[336,512]{1,0:T(8,128)(2,1)}, bf16[336,512]{1,0:T(8,128)(2,1)S(1)}, u32[]{:S(2)}, u32[]{:S(2)}) collective-permute-start(bf16[336,512]{1,0:T(8,128)(2,1)} %get-tuple-element.86), channel_id=1, source_target_pairs={{0,8},{8,0},{16,24},{24,16},{1,9},{9,1},{17,25},{25,17},{2,10},{10... | collective-permute-start | bytes 1032200 | tf_op jit(solution)/shard_map/ppermute | solution.py:419
  101.7 20.1 %collective-permute-start.16 = (bf16[336,512]{1,0:T(8,128)(2,1)}, bf16[336,512]{1,0:T(8,128)(2,1)S(1)}, u32[]{:S(2)}, u32[]{:S(2)}) collective-permute-start(bf16[336,512]{1,0:T(8,128)(2,1)} %get-tuple-element.87), channel_id=1, source_target_pairs={{0,16},{8,24},{16,0},{24,8},{1,17},{9,25},{17,1},{25,9},{2,18},{10... | collective-permute-start | bytes 1032200 | tf_op jit(solution)/shard_map/ppermute | solution.py:419
  102.3 21.4 %collective-permute-start.17 = (bf16[336,512]{1,0:T(8,128)(2,1)}, bf16[336,512]{1,0:T(8,128)(2,1)S(1)}, u32[]{:S(2)}, u32[]{:S(2)}) collective-permute-start(bf16[336,512]{1,0:T(8,128)(2,1)} %get-tuple-element.88), channel_id=1, source_target_pairs={{0,24},{8,16},{16,8},{24,0},{1,25},{9,17},{17,9},{25,1},{2,26},{10... | collective-permute-start | bytes 1032200 | tf_op jit(solution)/shard_map/ppermute | solution.py:419
  107.5 44.6 %collective-permute-start.28 = (bf16[64,4096]{1,0:T(8,128)(2,1)S(1)}, bf16[64,4096]{1,0:T(8,128)(2,1)S(1)}, u32[]{:S(2)}, u32[]{:S(2)}) collective-permute-start(bf16[64,4096]{1,0:T(8,128)(2,1)S(1)} %combine.4.refs_10_), channel_id=1, source_target_pairs={{0,4},{1,5},{2,6},{3,7},{4,0},{5,1},{6,2},{7,3},{8,12},{9,13},{10,... | collective-permute-start | bytes 1572872 | tf_op jit(solution)/shard_map/ppermute | solution.py:416
  120.1 11.2 %collective-permute-start.29 = (bf16[336,512]{1,0:T(8,128)(2,1)}, bf16[336,512]{1,0:T(8,128)(2,1)S(1)}, u32[]{:S(2)}, u32[]{:S(2)}) collective-permute-start(bf16[336,512]{1,0:T(8,128)(2,1)} %get-tuple-element.106), channel_id=1, source_target_pairs={{0,8},{8,0},{16,24},{24,16},{1,9},{9,1},{17,25},{25,17},{2,10},{10... | collective-permute-start | bytes 1032200 | tf_op jit(solution)/shard_map/ppermute | solution.py:419
  121.6 11.2 %collective-permute-start.30 = (bf16[336,512]{1,0:T(8,128)(2,1)}, bf16[336,512]{1,0:T(8,128)(2,1)S(1)}, u32[]{:S(2)}, u32[]{:S(2)}) collective-permute-start(bf16[336,512]{1,0:T(8,128)(2,1)} %get-tuple-element.107), channel_id=1, source_target_pairs={{0,16},{8,24},{16,0},{24,8},{1,17},{9,25},{17,1},{25,9},{2,18},{10... | collective-permute-start | bytes 1032200 | tf_op jit(solution)/shard_map/ppermute | solution.py:419
  121.8 16.1 %collective-permute-start.31 = (bf16[336,512]{1,0:T(8,128)(2,1)}, bf16[336,512]{1,0:T(8,128)(2,1)S(1)}, u32[]{:S(2)}, u32[]{:S(2)}) collective-permute-start(bf16[336,512]{1,0:T(8,128)(2,1)} %get-tuple-element.108), channel_id=1, source_target_pairs={{0,24},{8,16},{16,8},{24,0},{1,25},{9,17},{17,9},{25,1},{2,26},{10... | collective-permute-start | bytes 1032200 | tf_op jit(solution)/shard_map/ppermute | solution.py:419
  126.1 26.0 %collective-permute-start.27 = (bf16[64,4096]{1,0:T(8,128)(2,1)S(1)}, bf16[64,4096]{1,0:T(8,128)(2,1)S(1)}, u32[]{:S(2)}, u32[]{:S(2)}) collective-permute-start(bf16[64,4096]{1,0:T(8,128)(2,1)S(1)} %combine.5.refs_4_), channel_id=1, source_target_pairs={{0,6},{1,7},{2,0},{3,1},{4,2},{5,3},{6,4},{7,5},{8,14},{9,15},{10,... | collective-permute-start | bytes 1572872 | tf_op jit(solution)/shard_map/ppermute | solution.py:416
  131.3 10.7 %collective-permute-start.24 = (bf16[336,512]{1,0:T(8,128)(2,1)S(1)}, bf16[336,512]{1,0:T(8,128)(2,1)S(1)}, u32[]{:S(2)}, u32[]{:S(2)}) collective-permute-start(bf16[336,512]{1,0:T(8,128)(2,1)S(1)} %copy-done.22), channel_id=1, source_target_pairs={{0,8},{8,0},{16,24},{24,16},{1,9},{9,1},{17,25},{25,17},{2,10},{10... | collective-permute-start | bytes 1032200 | tf_op jit(solution)/shard_map/ppermute | solution.py:419
  139.5 12.7 %collective-permute-start.32 = (bf16[64,4096]{1,0:T(8,128)(2,1)S(1)}, bf16[64,4096]{1,0:T(8,128)(2,1)S(1)}, u32[]{:S(2)}, u32[]{:S(2)}) collective-permute-start(bf16[64,4096]{1,0:T(8,128)(2,1)S(1)} %combine.6), channel_id=1, source_target_pairs={{0,2},{1,3},{2,4},{3,5},{4,6},{5,7},{6,0},{7,1},{8,10},{9,11},{10,... | collective-permute-start | bytes 1572872 | tf_op jit(solution)/shard_map/ppermute | solution.py:416
  139.8 12.3 %collective-permute-start.25 = (bf16[336,512]{1,0:T(8,128)(2,1)S(1)}, bf16[336,512]{1,0:T(8,128)(2,1)S(1)}, u32[]{:S(2)}, u32[]{:S(2)}) collective-permute-start(bf16[336,512]{1,0:T(8,128)(2,1)S(1)} %copy-done.21), channel_id=1, source_target_pairs={{0,16},{8,24},{16,0},{24,8},{1,17},{9,25},{17,1},{25,9},{2,18},{10... | collective-permute-start | bytes 1032200 | tf_op jit(solution)/shard_map/ppermute | solution.py:419
  142.0 10.1 %collective-permute-start.26 = (bf16[336,512]{1,0:T(8,128)(2,1)S(1)}, bf16[336,512]{1,0:T(8,128)(2,1)S(1)}, u32[]{:S(2)}, u32[]{:S(2)}) collective-permute-start(bf16[336,512]{1,0:T(8,128)(2,1)S(1)} %copy-done.20), channel_id=1, source_target_pairs={{0,24},{8,16},{16,8},{24,0},{1,25},{9,17},{17,9},{25,1},{2,26},{10... | collective-permute-start | bytes 1032200 | tf_op jit(solution)/shard_map/ppermute | solution.py:419
  (31 other events, 229.5 us)
